TPU v7x, 512 devices: a whole 4x4x16 slice. The times are simulated.
512 devices in a mesh: dp: 64 (over x, z), seq: 8 (over y, core).
Axes of the slice: x: 4, y: 4, z: 16, core: 2. Of those that a mesh axis runs over, the one named last changes fastest.
Arguments:
- tokens: bfloat16 [131072, 1024], P(('dp', 'seq')), may hold values from -6 to 6
- teacher: float32 [131072], P(('dp', 'seq')), may hold values from -21 to 21
- cand_items: int32 [131072, 2], P(('dp', 'seq')), may hold values from 0 to 511, as said below
- owner_map: int32 [32768], P(('dp', 'seq')), may hold values from 0 to 63, as said below
- lengths: int32 [64], replicated, may hold values from 1 to 2048, 65536 in all
- w_proj: bfloat16 [1024, 2048], P('dp'), may hold values from -0.1875 to 0.1875
- w_out: bfloat16 [512, 1024], P('dp'), may hold values from -0.25 to 0.25
- gain_in: float32 [1024], replicated, may hold values from 0.5 to 1.5
- gain_mid: float32 [512], replicated, may hold values from 0.5 to 1.5
- item_table: bfloat16 [32768, 1024], P('dp'), may hold values from -0.1875 to 0.1875
Outputs:
- grad_tokens: bfloat16 [131072, 1024], P(('dp', 'seq'))
- loss: float32 [], replicated
Inputs may be any that keep to these rules, and one draw needn't show every extreme that they name: `owner_map`: the 64 entries held by each device name every index of dp once. `cand_items`: A row's two candidates are different items.
All inputs are finite; a program needn't handle non-finite values.
Results may differ from a plain program's by a relative error of at most 0.023.
Values may be sent and summed in bfloat16 or wider, within the bound.
A program may use at most 128 MiB of HBM per device.

v0:
```python
import jax
import jax.numpy as jnp
from jax import lax
from jax.sharding import PartitionSpec as P

HD = 128


epsilon = 1e-05


def as_sent(x):
    return jax.tree.map(lambda a: a.astype(jnp.bfloat16) if a.dtype == jnp.float32 else a, x)


def silu_slope(inputs):
    sigma = jax.nn.sigmoid(inputs)
    return sigma * (1.0 + inputs * (1.0 - sigma))


def normalize(inputs):
    centered = inputs - jnp.mean(inputs, axis=-1, keepdims=True)
    factor = lax.rsqrt(jnp.mean(centered * centered, axis=-1, keepdims=True) + epsilon)
    return (centered * factor, factor)


def normalize_back(upstream, normed, factor):
    inner = jnp.mean(upstream * normed, axis=-1, keepdims=True)
    return (upstream - jnp.mean(upstream, axis=-1, keepdims=True) - normed * inner) * factor


def split_heads(inputs, head_count):
    return inputs.reshape(inputs.shape[0], head_count, inputs.shape[1] // head_count)


def tile_scores(query_rows, key_rows, query_pos, key_pos, live_length, head_count):
    scores = jnp.einsum(
        "qhd,khd->hqk",
        split_heads(query_rows, head_count),
        split_heads(key_rows, head_count),
        preferred_element_type=jnp.float32,
    ) * HD ** (-0.5)
    mask = ((key_pos[None, :] <= query_pos[:, None]) & (key_pos[None, :] < live_length)).astype(
        jnp.float32
    )
    return (scores, mask[None, :, :])


def fold_pieces(update, initial, whole, row_count):
    count = whole[0].shape[0] // row_count

    def step(index, running):
        offset = index * row_count
        segment = tuple((lax.dynamic_slice_in_dim(array, offset, row_count, 0) for array in whole))
        return update(running, segment, offset)

    return lax.fori_loop(0, count, step, initial)


def on_device(
    tokens, teacher, cand_items, owner_map, lengths, w_proj, w_out, gain_in, gain_mid, item_table
):
    row_count, model_width = tokens.shape
    group_count = lax.axis_size("dp")
    part_count = lax.axis_size("seq")
    history = row_count * part_count
    seq_place = lax.axis_index("seq")
    live_length = lengths[lax.axis_index("dp")]
    live_total = jnp.sum(lengths).astype(jnp.float32)
    head_width = w_out.shape[0] * group_count
    head_count = head_width // HD
    block_rows = row_count // group_count
    own_pos = seq_place * row_count + jnp.arange(row_count)
    first_query = jnp.min(own_pos)
    last_query = jnp.max(own_pos)
    alive_rows = (own_pos < live_length).astype(jnp.float32)
    bucket_order = jnp.argsort(owner_map)

    def bucket(inputs):
        return jnp.take(
            inputs.reshape((group_count, block_rows) + inputs.shape[1:]), bucket_order, axis=0
        )

    w_full, w_back = (
        lax.all_gather(w_proj, "dp", axis=0, tiled=True),
        lax.all_gather(w_out, "dp", axis=0, tiled=True),
    )
    normed_raw, factor_in = normalize(tokens.astype(jnp.float32))
    normed_in = (normed_raw * gain_in).astype(jnp.bfloat16)
    projected = jnp.dot(normed_in, w_full, preferred_element_type=jnp.float32)
    activated = jax.nn.silu(projected).astype(jnp.bfloat16)
    gate_rows = activated[:, :head_width]
    value_rows = activated[:, head_width : 2 * head_width]
    query_rows = activated[:, 2 * head_width : 3 * head_width]
    key_rows = activated[:, 3 * head_width :]
    key_whole, value_whole = (
        lax.all_gather(key_rows, "seq", axis=0, tiled=True),
        lax.all_gather(value_rows, "seq", axis=0, tiled=True),
    )
    zeros_rows = jnp.zeros((row_count, head_width), jnp.float32)

    def forward_piece(running, segment, offset):
        key_piece, value_piece = segment
        key_pos = offset + jnp.arange(key_piece.shape[0])

        def forward_compute(current):
            scores, mask = tile_scores(
                query_rows, key_piece, own_pos, key_pos, live_length, head_count
            )
            weights = (jax.nn.silu(scores) * (mask / history)).astype(jnp.bfloat16)
            product = jnp.einsum(
                "hqk,khd->qhd",
                weights,
                split_heads(value_piece, head_count),
                preferred_element_type=jnp.float32,
            )
            return current + product.reshape(row_count, head_width)

        first_key = jnp.min(key_pos)
        useful = (first_key <= last_query) & (first_key < live_length)
        return lax.cond(useful, forward_compute, lambda current: current, running)

    attended = fold_pieces(forward_piece, zeros_rows, (key_whole, value_whole), row_count)
    normed_mid, factor_mid = normalize(attended)
    gated = (normed_mid * gain_mid * gate_rows.astype(jnp.float32)).astype(jnp.bfloat16)
    layer_out = (
        tokens.astype(jnp.float32) + jnp.dot(gated, w_back, preferred_element_type=jnp.float32)
    ).astype(jnp.bfloat16)
    out_rows = lax.all_to_all(bucket(layer_out), "dp", split_axis=0, concat_axis=0, tiled=True)
    item_ids = lax.all_to_all(bucket(cand_items), "dp", split_axis=0, concat_axis=0, tiled=True)
    target = lax.all_to_all(
        bucket(teacher).astype(jnp.bfloat16), "dp", split_axis=0, concat_axis=0, tiled=True
    ).astype(jnp.float32)
    alive = lax.all_to_all(
        bucket(alive_rows).astype(jnp.bfloat16), "dp", split_axis=0, concat_axis=0, tiled=True
    ).astype(jnp.float32)
    pos_rows = jnp.take(item_table, item_ids[..., 0], axis=0).astype(jnp.float32)
    neg_rows = jnp.take(item_table, item_ids[..., 1], axis=0).astype(jnp.float32)
    difference = pos_rows - neg_rows
    misses = (jnp.sum(out_rows.astype(jnp.float32) * difference, axis=-1) - target) * alive
    grad_rows = (2.0 / live_total * misses[..., None] * difference).astype(jnp.bfloat16)
    grad_back = lax.all_to_all(grad_rows, "dp", split_axis=0, concat_axis=0, tiled=True)
    squared = lax.all_to_all(
        as_sent(misses * misses), "dp", split_axis=0, concat_axis=0, tiled=True
    )
    grad_out = jnp.take(grad_back, owner_map, axis=0).reshape(row_count, model_width)
    loss_part = jnp.sum(squared)
    loss = lax.psum(loss_part, ("dp", "seq")) / live_total
    grad_gated = jnp.dot(grad_out, w_back.T, preferred_element_type=jnp.float32)
    grad_gate = grad_gated * normed_mid * gain_mid
    grad_normed = grad_gated * gain_mid * gate_rows.astype(jnp.float32)
    grad_attended = normalize_back(grad_normed, normed_mid, factor_mid).astype(jnp.bfloat16)
    slope_scale = HD ** (-0.5) / history

    def query_piece(running, segment, offset):
        key_piece, value_piece = segment
        key_pos = offset + jnp.arange(key_piece.shape[0])

        def query_compute(current):
            scores, mask = tile_scores(
                query_rows, key_piece, own_pos, key_pos, live_length, head_count
            )
            grad_weights = jnp.einsum(
                "qhd,khd->hqk",
                split_heads(grad_attended, head_count),
                split_heads(value_piece, head_count),
                preferred_element_type=jnp.float32,
            )
            grad_scores = (grad_weights * silu_slope(scores) * (mask * slope_scale)).astype(
                jnp.bfloat16
            )
            product = jnp.einsum(
                "hqk,khd->qhd",
                grad_scores,
                split_heads(key_piece, head_count),
                preferred_element_type=jnp.float32,
            )
            return current + product.reshape(row_count, head_width)

        first_key = jnp.min(key_pos)
        useful = (first_key <= last_query) & (first_key < live_length)
        return lax.cond(useful, query_compute, lambda current: current, running)

    grad_query = fold_pieces(query_piece, zeros_rows, (key_whole, value_whole), row_count)
    query_piece_rows = lax.all_gather(query_rows, "seq", axis=0, tiled=True)
    grad_piece = lax.all_gather(grad_attended, "seq", axis=0, tiled=True)
    piece_pos = jnp.arange(query_piece_rows.shape[0])

    def key_compute(current):
        scores, mask = tile_scores(
            query_piece_rows, key_rows, piece_pos, own_pos, live_length, head_count
        )
        weights = (jax.nn.silu(scores) * (mask / history)).astype(jnp.bfloat16)
        grad_heads = split_heads(grad_piece, head_count)
        grad_weights = jnp.einsum(
            "qhd,khd->hqk",
            grad_heads,
            split_heads(value_rows, head_count),
            preferred_element_type=jnp.float32,
        )
        grad_scores = (grad_weights * silu_slope(scores) * (mask * slope_scale)).astype(
            jnp.bfloat16
        )
        key_part = jnp.einsum(
            "hqk,qhd->khd",
            grad_scores,
            split_heads(query_piece_rows, head_count),
            preferred_element_type=jnp.float32,
        )
        value_part = jnp.einsum(
            "hqk,qhd->khd", weights, grad_heads, preferred_element_type=jnp.float32
        )
        return (key_part.reshape(row_count, head_width), value_part.reshape(row_count, head_width))

    useful = (jnp.max(piece_pos) >= first_query) & (first_query < live_length)
    grad_key, grad_value = lax.cond(
        useful, key_compute, lambda current: current, (zeros_rows, zeros_rows)
    )
    grad_proj = jnp.concatenate([grad_gate, grad_value, grad_query, grad_key], axis=1)
    grad_pre = (grad_proj * silu_slope(projected)).astype(jnp.bfloat16)
    grad_in = jnp.dot(grad_pre, w_full.T, preferred_element_type=jnp.float32)
    grad_tokens = (
        grad_out.astype(jnp.float32) + normalize_back(grad_in * gain_in, normed_raw, factor_in)
    ).astype(jnp.bfloat16)
    return (grad_tokens, loss)


def solution(mesh):
    in_specs = (
        P(("dp", "seq"), None),
        P(("dp", "seq")),
        P(("dp", "seq"), None),
        P(("dp", "seq")),
        P(),
        P("dp", None),
        P("dp", None),
        P(),
        P(),
        P("dp", None),
    )
    out_specs = (P(("dp", "seq"), None), P())
    return jax.shard_map(
        on_device, mesh=mesh, in_specs=in_specs, out_specs=out_specs, check_vma=False
    )
```

profile of v0, /device:TPU:25, one launch (start us, length us, event | category | flops | bytes accessed | tf_op | source)
XLA Modules:
  0.0 715.4 jit_solution(10008878670132380583)
XLA Ops:
  10.5 143.1 %all-gather.7.cloned.1.call-done = bf16[1024,2048]{1,0:T(8,128)(2,1)} async-done(((bf16[16,2048]{1,0:T(8,128)(2,1)}), bf16[1024,2048]{1,0:T(8,128)(2,1)}) %all-gather.7.cloned.1.call-update) | async-done | bytes 4194320 | tf_op jit(solution)/shard_map/all_gather | solution.py:85
  153.6 5.1 multiply_convert_fusion.4
  167.6 8.4 %all-to-all-start.2 = ((bf16[64,1,4]{2,1,0:T(2,128)(2,1)}), bf16[64,1,4]{2,1,0:T(2,128)(2,1)S(1)}, u32[]{:S(2)}, u32[]{:S(2)}) async-start(bf16[64,1,4]{2,1,0:T(2,128)(2,1)} %copy.110), calls=%async_computation.2 | async-start | bytes 65536 | tf_op jit(solution)/shard_map/all_to_all | solution.py:131
  178.9 16.8 %all-gather.11.cloned.1.call-done = bf16[2048,512]{1,0:T(8,128)(2,1)} async-done(((bf16[256,512]{1,0:T(8,128)(2,1)}), bf16[2048,512]{1,0:T(8,128)(2,1)}) %all-gather.11.cloned.1.call-update) | async-done | bytes 2097168 | tf_op jit(solution)/shard_map/all_gather | solution.py:98
  199.7 31.5 %all-gather.9.cloned.1.call-done = bf16[2048,512]{1,0:T(8,128)(2,1)} async-done(((bf16[256,512]{1,0:T(8,128)(2,1)}), bf16[2048,512]{1,0:T(8,128)(2,1)}) %all-gather.9.cloned.1.call-update) | async-done | bytes 2097168 | tf_op jit(solution)/shard_map/all_gather | solution.py:97
  231.2 4.0 copy.106
  235.2 54.8 %while.34 = (s32[]{:T(128)}, f32[256,512]{0,1:T(8,128)S(1)}, s32[]{:T(128)}, s32[]{:T(128)}, bf16[2048,512]{0,1:T(8,128)(2,1)}, /*index=5*/bf16[256,512]{1,0:T(8...) while((s32[]{:T(128)}, f32[256,512]{0,1:T(8,128)S(1)}, s32[]{:T(128)}, ...), condition=%wide.region_8.9_spmd.clone, body=%wide.region_4.8_spmd.clone.sunk | while | flops 136381440 | bytes 4464401 | solution.py:57
  290.6 14.2 %all-to-all-start.3 = ((bf16[64,1,4]{2,1,0:T(2,128)(2,1)}), bf16[64,1,4]{2,1,0:T(2,128)(2,1)S(1)}, u32[]{:S(2)}, u32[]{:S(2)}) async-start(bf16[64,1,4]{2,1,0:T(2,128)(2,1)} %copy.112), calls=%async_computation.3 | async-start | bytes 65536 | tf_op jit(solution)/shard_map/all_to_all | solution.py:134
  304.8 59.6 %all-gather.13.cloned.1.call-done = bf16[512,1024]{1,0:T(8,128)(2,1)} async-done(((bf16[8,1024]{1,0:T(8,128)(2,1)}), bf16[512,1024]{1,0:T(8,128)(2,1)}) %all-gather.13.cloned.1.call-update) | async-done | bytes 1048592 | tf_op jit(solution)/shard_map/all_gather | solution.py:86
  367.5 9.0 %all-to-all-start.1 = ((s32[64,4,2]{1,2,0:T(2,128)}), s32[64,4,2]{1,2,0:T(2,128)S(1)}, u32[]{:S(2)}, u32[]{:S(2)}) async-start(s32[64,4,2]{1,2,0:T(2,128)} %broadcast_select_fusion.4), calls=%async_computation.1 | async-start | bytes 131072 | tf_op jit(solution)/shard_map/all_to_all | solution.py:130
  377.7 12.4 %all-to-all-done.1 = s32[64,4,2]{1,2,0:T(2,128)S(1)} async-done(((s32[64,4,2]{1,2,0:T(2,128)}), s32[64,4,2]{1,2,0:T(2,128)S(1)}, u32[]{:S(2)}, u32[]{:S(2)}) %all-to-all-start.1) | async-done | bytes 2080 | tf_op jit(solution)/shard_map/all_to_all | solution.py:130
  390.0 4.6 all-to-all-start
  401.3 14.2 %all-to-all-done = bf16[64,4,1024]{2,1,0:T(4,128)(2,1)S(1)} async-done(((bf16[64,4,1024]{2,1,0:T(4,128)(2,1)}), bf16[64,4,1024]{2,1,0:T(4,128)(2,1)S(1)}, u32[]{:S(2)}, u32[]{:S(2)}) %all-to-all-start) | async-done | bytes 524320 | tf_op jit(solution)/shard_map/all_to_all | solution.py:129
  417.9 6.6 all-to-all-start.4
  424.6 20.5 %all-to-all-done.4 = bf16[64,4,1024]{2,1,0:T(4,128)(2,1)S(1)} async-done(((bf16[64,4,1024]{2,1,0:T(4,128)(2,1)}), bf16[64,4,1024]{2,1,0:T(4,128)(2,1)S(1)}, u32[]{:S(2)}, u32[]{:S(2)}) %all-to-all-start.4) | async-done | bytes 524320 | tf_op jit(solution)/shard_map/all_to_all | solution.py:142
  454.8 6.7 all-to-all-start.5
  464.1 10.7 %all-to-all-done.5 = bf16[64,1,4]{2,1,0:T(2,128)(2,1)S(1)} async-done(((bf16[64,1,4]{2,1,0:T(2,128)(2,1)}), bf16[64,1,4]{2,1,0:T(2,128)(2,1)S(1)}, u32[]{:S(2)}, u32[]{:S(2)}) %all-to-all-start.5) | async-done | bytes 544 | tf_op jit(solution)/shard_map/all_to_all | solution.py:143
  475.4 113.8 %psum.7 = bf16[]{:T(256)} all-reduce(bf16[]{:T(256)} %reduce_sum.115), channel_id=1, replica_groups=mesh['dp'=64,'seq'=8] {'dp','seq'}, use_global_device_ids=true, to_apply=%region_26.30 | all-reduce | flops 1 | bytes 4 | tf_op jit(solution)/shard_map/psum | solution.py:148
  589.8 76.4 %while.35 = (s32[]{:T(128)}, f32[256,512]{0,1:T(8,128)S(1)}, s32[]{:T(128)}, s32[]{:T(128)}, bf16[2048,512]{0,1:T(8,128)(2,1)}, /*index=5*/bf16[256,512]{1,0:T(8...) while((s32[]{:T(128)}, f32[256,512]{0,1:T(8,128)S(1)}, ...), condition=%wide.region_22.26_spmd.clone, body=%wide.region_18.25_spmd.clone.sunk | while | flops 204538880 | bytes 7085857 | solution.py:57
  592.9 6.5 conditional.9
  602.4 6.5 conditional.9
  612.0 6.5 conditional.9
  621.5 6.5 conditional.9
  631.1 6.5 conditional.9
  640.6 6.5 conditional.9
  650.2 6.5 conditional.9
  659.7 6.5 conditional.9
  667.3 34.1 %conditional.3 = (f32[256,512]{1,0:T(8,128)S(1)}, f32[256,512]{1,0:T(8,128)S(1)}) conditional(s32[]{:T(128)} %convert_element_type.153, () %tuple.86, (bf16[2048,512]{1,0:T(8,128)(2,1)}, bf16[256,512]{1,0:T(8,128)(2,1)}, bf16[2048,512]{1,0:T(8,128)(2,1)}, bf16[256,512]{1,0:T(8,128)(2,1)}, s32[256]{0:T(256)S(1)}, /*index=5*/s32[2048]{0:T(1024)S(1)}, ...), branch_computations={%region_16.20_spmd, %region_17.21_spmd} | conditional | flops 2187329792 | bytes 64498280 | solution.py:216
  678.7 4.5 fusion.23
  683.2 10.5 %fusion.18 = f32[4,256,128]{1,2,0:T(8,128)} fusion(bf16[2048,4,128]{0,2,1:T(8,128)(2,1)} %bitcast.109, f32[4,2048,256]{2,1,0:T(8,128)} %fusion.23, bf16[2048,4,128]{0,2,1:T(8,128)(2,1)} %bitcast.114, f32[2048,256]{1,0:T(8,128)} %get-tuple-element.735, bf16[256,512]{1,0:T(8,128)(2,1)S(1)} %copy-done.9), kind=kOutput, calls=%fused_computation.33 | convolution fusion | flops 1096810496 | bytes 15466496 | tf_op jit(solution)/shard_map/cond/branch_1_fun/hqk,qhd->khd/dot_general | solution.py:204
  693.6 6.3 fusion.15
  701.4 4.8 fusion.88
  (273 shorter events, 177.0 us)
Async XLA Ops:
  7.2 389.5 %copy-start = (bf16[512,1024]{1,0:T(8,128)(2,1)S(1)}, bf16[512,1024]{1,0:T(8,128)(2,1)}, u32[]{:S(2)}) copy-start(bf16[512,1024]{1,0:T(8,128)(2,1)} %param.35) | copy-start | bytes 3145732
  7.2 146.4 %all-gather.7.cloned.1.call-start = ((), (), s32[]{:S(2)}) async-start(), calls=%async_computation.6 | async-start | bytes 4259840 | tf_op jit(solution)/shard_map/all_gather | solution.py:85
  7.9 187.8 %all-gather.11.cloned.1.call-start = ((), (), s32[]{:S(2)}) async-start(), calls=%async_computation.8 | async-start | bytes 2359296 | tf_op jit(solution)/shard_map/all_gather | solution.py:98
  158.7 1.0 copy-start.7
  158.7 3.3 copy-start.16
  158.7 5.3 copy-start.15
  158.7 6.7 copy-start.13
  158.7 18.6 %copy-start.12 = (s32[256,2]{0,1:T(2,128)S(1)}, s32[256,2]{0,1:T(2,128)}, u32[]{:S(2)}) copy-start(s32[256,2]{0,1:T(2,128)} %param.28) | copy-start | bytes 6148
  160.6 70.5 %all-gather.9.cloned.1.call-start = ((), (), s32[]{:S(2)}) async-start(), calls=%async_computation.7 | async-start | bytes 2359296 | tf_op jit(solution)/shard_map/all_gather | solution.py:97
  161.3 203.1 %all-gather.13.cloned.1.call-start = ((), (), s32[]{:S(2)}) async-start(), calls=%async_computation.9 | async-start | bytes 1064960 | tf_op jit(solution)/shard_map/all_gather | solution.py:86
  167.6 123.0 %all-to-all-start.2 = ((bf16[64,1,4]{2,1,0:T(2,128)(2,1)}), bf16[64,1,4]{2,1,0:T(2,128)(2,1)S(1)}, u32[]{:S(2)}, u32[]{:S(2)}) async-start(bf16[64,1,4]{2,1,0:T(2,128)(2,1)} %copy.110), calls=%async_computation.2 | async-start | bytes 65536 | tf_op jit(solution)/shard_map/all_to_all | solution.py:131
  290.0 74.4 %copy-start.1 = (bf16[256,1024]{1,0:T(8,128)(2,1)S(1)}, bf16[256,1024]{1,0:T(8,128)(2,1)}, u32[]{:S(2)}) copy-start(bf16[256,1024]{1,0:T(8,128)(2,1)} %param.26) | copy-start | bytes 1572868
  290.0 74.4 %copy-start.11 = (f32[512]{0:T(512)S(1)}, f32[512]{0:T(512)}, u32[]{:S(2)}) copy-start(f32[512]{0:T(512)} %param.34) | copy-start | bytes 6148
  290.6 76.9 %all-to-all-start.3 = ((bf16[64,1,4]{2,1,0:T(2,128)(2,1)}), bf16[64,1,4]{2,1,0:T(2,128)(2,1)S(1)}, u32[]{:S(2)}, u32[]{:S(2)}) async-start(bf16[64,1,4]{2,1,0:T(2,128)(2,1)} %copy.112), calls=%async_computation.3 | async-start | bytes 65536 | tf_op jit(solution)/shard_map/all_to_all | solution.py:134
  367.5 22.5 %all-to-all-start.1 = ((s32[64,4,2]{1,2,0:T(2,128)}), s32[64,4,2]{1,2,0:T(2,128)S(1)}, u32[]{:S(2)}, u32[]{:S(2)}) async-start(s32[64,4,2]{1,2,0:T(2,128)} %broadcast_select_fusion.4), calls=%async_computation.1 | async-start | bytes 131072 | tf_op jit(solution)/shard_map/all_to_all | solution.py:130
  390.0 25.5 %all-to-all-start = ((bf16[64,4,1024]{2,1,0:T(4,128)(2,1)}), bf16[64,4,1024]{2,1,0:T(4,128)(2,1)S(1)}, u32[]{:S(2)}, u32[]{:S(2)}) async-start(bf16[64,4,1024]{2,1,0:T(4,128)(2,1)} %broadcast_select_fusion.1), calls=%async_computation | async-start | bytes 1048576 | tf_op jit(solution)/shard_map/all_to_all | solution.py:129
  394.7 272.5 %all-gather.17.cloned.1.call-start = ((), (), s32[]{:S(2)}) async-start(), calls=%async_computation.11 | async-start | bytes 2359296 | tf_op jit(solution)/shard_map/all_gather | solution.py:185
  417.9 32.3 %copy-start.6 = (bf16[512,1024]{1,0:T(8,128)(2,1)S(1)}, bf16[512,1024]{1,0:T(8,128)(2,1)}, u32[]{:S(2)}) copy-start(bf16[512,1024]{1,0:T(8,128)(2,1)} %all-gather.13.cloned.1.call-done) | copy-start | bytes 3145732
  417.9 27.2 %all-to-all-start.4 = ((bf16[64,4,1024]{2,1,0:T(4,128)(2,1)}), bf16[64,4,1024]{2,1,0:T(4,128)(2,1)S(1)}, u32[]{:S(2)}, u32[]{:S(2)}) async-start(bf16[64,4,1024]{2,1,0:T(4,128)(2,1)} %multiply_convert_fusion.5), calls=%async_computation.4 | async-start | bytes 1048576 | tf_op jit(solution)/shard_map/all_to_all | solution.py:142
  424.5 242.7 %all-gather.15.cloned.1.call-start = ((), (), s32[]{:S(2)}) async-start(), calls=%async_computation.10 | async-start | bytes 2359296 | tf_op jit(solution)/shard_map/all_gather | solution.py:186
  450.2 3.9 copy-start.4
  454.8 20.0 %all-to-all-start.5 = ((bf16[64,1,4]{2,1,0:T(2,128)(2,1)}), bf16[64,1,4]{2,1,0:T(2,128)(2,1)S(1)}, u32[]{:S(2)}, u32[]{:S(2)}) async-start(bf16[64,1,4]{2,1,0:T(2,128)(2,1)} %multiply_convert_fusion.7), calls=%async_computation.5 | async-start | bytes 65536 | tf_op jit(solution)/shard_map/all_to_all | solution.py:143
  667.2 34.1 %copy-start.2 = (bf16[256,1024]{1,0:T(8,128)(2,1)S(1)}, bf16[256,1024]{1,0:T(8,128)(2,1)}, u32[]{:S(2)}) copy-start(bf16[256,1024]{1,0:T(8,128)(2,1)} %param.26) | copy-start | bytes 1572868
  667.2 34.1 %copy-start.10 = (f32[256,512]{1,0:T(8,128)S(1)}, f32[256,512]{1,0:T(8,128)}, u32[]{:S(2)}) copy-start(f32[256,512]{1,0:T(8,128)} %get-tuple-element.743) | copy-start | bytes 1572868
  667.2 34.1 %copy-start.14 = (f32[1024]{0:T(1024)S(1)}, f32[1024]{0:T(1024)}, u32[]{:S(2)}) copy-start(f32[1024]{0:T(1024)} %param.33) | copy-start | bytes 12292
  676.1 2.4 copy-start.3
  676.1 2.5 copy-start.8
  678.7 4.5 copy-start.9
  701.4 4.8 copy-start.5
Sparse Core Ops, SparseCore 0:
  11.0 142.6 all-gather.6
  160.7 34.9 all-gather.10
  197.9 33.2 all-gather.8
  233.9 130.4 all-gather.12
  401.4 45.0 all-gather.16
  454.2 38.9 all-gather.14
where the time goes:
time: 718 us; the launch traced here: 715 us
  waiting for transfers between devices  311 us (43%)
  blocking collectives  114 us (16%)
  matrix products  72.5 us (10%)
  local copies, waits for them, and re-layouts  56.7 us (8%)
  other arithmetic  51.5 us (7%)
  starting transfers between devices  50 us (7%)
  loops' own time  41.2 us (6%)
  between operations  19 us (3%)
    all_gather x1, waiting for transfers between devices, on_device(): lax.all_gather(w_proj, 'dp', axis=0, tiled=True)  143 us
    psum x1, blocking collectives, on_device(): loss = lax.psum(loss_part, ('dp', 'seq')) / live_total  114 us
    all_gather x1, waiting for transfers between devices, on_device(): lax.all_gather(w_out, 'dp', axis=0, tiled=True)  59.6 us
    another operation x2, loops' own time, fold_pieces(): return lax.fori_loop(0, count, step, initial)  40 us
    all_gather x1, waiting for transfers between devices, on_device(): lax.all_gather(key_rows, 'seq', axis=0, tiled=True)  31.5 us
    dynamic_slice x16, local copies, waits for them, and re-layouts, step(): lax.dynamic_slice_in_dim(array, offset, row_count, 0)  22.8 us
    all_to_all x1, waiting for transfers between devices, on_device(): lax.all_to_all(grad_rows, 'dp', split_axis=0, concat_axis=0, tiled=True)  20.5 us
    all_gather x1, waiting for transfers between devices, on_device(): lax.all_gather(value_rows, 'seq', axis=0, tiled=True)  16.8 us
  transfers between devices with their start and end apart: 12, of which 8 were waited for; matrix products, arithmetic and copies ran while one was open for 19% of the time, Pallas kernels for 0%

commit v1 on v0

v1 whole, which is shorter than its diff:
```python
import functools

import jax
import jax.numpy as jnp
from jax import lax
from jax.experimental import pallas as pl
from jax.experimental.pallas import tpu as pltpu
from jax.sharding import PartitionSpec as P

MESH = pl.DeviceIdType.MESH
F32 = jnp.float32
BF16 = jnp.bfloat16
HEADS = 4
NZ = 16
CORES = 2
TILE = 16
EPSILON = 1e-05


def dot(a, b):
    return jnp.dot(a, b, preferred_element_type=F32)


def dot_nt(a, b):
    return lax.dot_general(a, b, (((1,), (1,)), ((), ())), preferred_element_type=F32)


def iota(shape, axis):
    return lax.broadcasted_iota(jnp.int32, shape, axis)


def one_hot(condition):
    return jnp.where(condition, 1.0, 0.0).astype(BF16)


def silu_slope(inputs):
    sigma = jax.nn.sigmoid(inputs)
    return sigma * (1.0 + inputs * (1.0 - sigma))


def normalize(inputs):
    centered = inputs - jnp.mean(inputs, axis=-1, keepdims=True)
    factor = lax.rsqrt(jnp.mean(centered * centered, axis=-1, keepdims=True) + EPSILON)
    return (centered * factor, factor)


def normalize_back(upstream, normed, factor):
    inner = jnp.mean(upstream * normed, axis=-1, keepdims=True)
    return (upstream - jnp.mean(upstream, axis=-1, keepdims=True) - normed * inner) * factor


def small_parts(values):
    whole = values.astype(jnp.int32)
    return (whole >> 4).astype(F32).astype(BF16), (whole & 15).astype(F32).astype(BF16)


def pair(t, u, parity):
    return t * (t + 1) + 2 * u + parity


def kernel(
    tok_ref, teach_ref, cand_ref, own_ref, len_ref, wp_ref, wo_ref, gin_ref, gmid_ref, table_hbm,
    out_ref, loss_ref,
    wall, xn, table, req_send, req_recv, rq, dsend, drecv, idiff, proj, kv, kt, vt, qs, qt, wst, slope,
    att_send, att_recv, gproj, wout, gout, gpg, da_send, da_recv, dat, dvk_send, dvk_recv, dqt,
    gps, gpr, lb0, lb1, lb2,
    lsem, xs, xr, zs, zr, rs, rr, ts, tr, req_s, req_r, dif_s, dif_r,
    ws, wr, wrs, wrr, vs, vr, vrs, vrr, ks, kr, as_, ar, gs, gr, ps, pr, fs, fr, l0s, l0r, l1s, l1r, l2s, l2r,
):
    rows, width = tok_ref.shape
    hd = kv.shape[2] // 2
    ndp = req_send.shape[0]
    nx = ndp // NZ
    nseq = HEADS * CORES
    half = NZ // 2
    cap = rows // ndp
    quarter = width // 4
    history = rows * nseq
    scale = float(hd) ** -0.5

    dp = lax.axis_index("dp")
    sq = lax.axis_index("seq")
    x, z = lax.div(dp, NZ), lax.rem(dp, NZ)
    y, c = lax.div(sq, CORES), lax.rem(sq, CORES)
    other = 1 - c
    way = 1 - 2 * c
    yp, ym = lax.rem(y + 1, HEADS), lax.rem(y + HEADS - 1, HEADS)
    yo = lax.rem(y + 2, HEADS)
    up, down = (dp, yp * CORES + c), (dp, ym * CORES + c)
    sibling = (dp, y * CORES + other)

    def rcopy(src, dst, send, recv, device):
        return pltpu.make_async_remote_copy(
            src_ref=src, dst_ref=dst, send_sem=send, recv_sem=recv, device_id=device, device_id_type=MESH
        )

    barrier = pltpu.get_barrier_semaphore()

    def greet(i, carry):
        pl.semaphore_signal(barrier, inc=1, device_id=(lax.rem(dp + i, ndp), sq), device_id_type=MESH)
        return carry

    lax.fori_loop(1, ndp, greet, 0)
    for d in range(1, nseq):
        pl.semaphore_signal(barrier, inc=1, device_id=(dp, lax.rem(sq + d, nseq)), device_id_type=MESH)

    hw = HEADS * hd
    pieces = [
        (wo_ref, 0, 0),
        (wp_ref, 0, hd),
        (wp_ref, hw, 2 * hd),
        (wp_ref, 3 * hw, 3 * hd),
        (wp_ref, 2 * hw, 4 * hd),
    ]
    local = []
    for i, (src, start, to) in enumerate(pieces):
        begin = pl.multiple_of(start + y * hd, hd)
        local.append(
            pltpu.make_async_copy(src.at[:, pl.ds(begin, hd)], wall.at[y, x, z, :, pl.ds(to, hd)], lsem.at[i])
        )
    table_copy = pltpu.make_async_copy(table_hbm, table, lsem.at[5])
    for copy in local:
        copy.start()
    table_copy.start()

    tokens = tok_ref[...].astype(F32)
    normed_raw, factor_in = normalize(tokens)
    xn[y] = (normed_raw * gin_ref[...]).astype(BF16)

    own_row = own_ref[...]
    expand = one_hot(lax.div(iota((ndp, rows), 1), cap) == iota((ndp, rows), 0))
    own_rep = dot(jnp.broadcast_to(own_row.astype(F32).astype(BF16), (8, ndp)), expand)[0:1, :]
    to_owner = one_hot(iota((ndp, rows), 0).astype(F32) == own_rep)
    lane = iota((128, rows), 0)
    inside = (lax.div(lane, 2) == lax.rem(iota((128, rows), 1), cap)) & (lane < 2 * cap)
    both = jnp.where(lax.rem(lane, 2) == 0, cand_ref[0:1, :], cand_ref[1:2, :])
    high, low = small_parts(jnp.where(inside, both, 0))
    requests = dot_nt(to_owner, high) * 16.0 + dot_nt(to_owner, low)
    for p in range(ndp):
        req_send[p] = requests[p : p + 1, :]

    for copy in local:
        copy.wait()
    pl.semaphore_wait(barrier, ndp - 1 + nseq - 1)

    x_copies = []
    for d in range(1, nx):
        device = (lax.rem(x + d, nx) * NZ + z, sq)
        copy = rcopy(wall.at[y, x, z], wall.at[y, x, z], xs.at[d - 1], xr.at[d - 1], device)
        copy.start()
        x_copies.append(copy)

    def y_copies(part, send, recv):
        return [
            rcopy(part(y, 0), part(y, 0), send.at[0], recv.at[0], up),
            rcopy(part(y, 1), part(y, 1), send.at[1], recv.at[1], down),
            rcopy(part(y, 1), part(y, 1), send.at[2], recv.at[2], up),
            rcopy(part(y, 0), part(y, 0), send.at[3], recv.at[3], down),
            rcopy(part(ym, 0), part(ym, 0), send.at[4], recv.at[4], up),
            rcopy(part(yp, 1), part(yp, 1), send.at[5], recv.at[5], down),
        ]

    def y_start(copies):
        for copy in copies[:4]:
            copy.start()

    def y_forward(copies):
        copies[0].wait_recv()
        copies[4].start()
        copies[1].wait_recv()
        copies[5].start()

    tok_copies = y_copies(lambda at, h: xn.at[at, pl.ds(h * (rows // 2), rows // 2), :], ts, tr)
    y_start(tok_copies)

    def send_request(i, carry):
        p = lax.rem(dp + i, ndp)
        rcopy(req_send.at[p], req_recv.at[dp], req_s, req_r, (p, sq)).start()
        return carry

    lax.fori_loop(1, ndp, send_request, 0)
    req_recv[dp] = req_send[dp]

    def at_z(distance):
        return lax.rem(z - way * distance + NZ, NZ)

    ahead = (x * NZ + lax.rem(z + way + NZ, NZ), sq)
    z_copies, relays = [], []
    for k in range(half):
        src = wall.at[y, :, at_z(k)]
        z_copies.append(rcopy(src, src, zs.at[k], zr.at[k], ahead))
        if k < half - 1:
            got = wall.at[y, :, at_z(k + 1)]
            relays.append(rcopy(got, got, rs.at[k], rr.at[k], sibling))

    def ring_step(k):
        z_copies[k].wait_recv()
        if k + 1 < half:
            z_copies[k + 1].start()
            relays[k].start()

    for copy in x_copies:
        copy.wait_recv()
    z_copies[0].start()
    first = min(2, half)
    for k in range(first):
        ring_step(k)

    bulk = pl.ds(0, ndp - 1)
    neighbour = (lax.rem(dp + 1, ndp), sq)
    request_bulk = rcopy(req_send.at[bulk], req_recv.at[bulk], req_s, req_r, neighbour)
    request_bulk.wait_recv()
    for p in range(ndp):
        rq[p : p + 1, :] = req_recv[p]
    table_copy.wait()
    high, low = small_parts(rq[...])
    chunk = ndp * TILE // 4
    per = chunk // TILE
    for part in range(4):
        row = iota((chunk, 128), 0)
        spread = one_hot(lax.div(iota((chunk, ndp), 0), TILE) + part * per == iota((chunk, ndp), 1))
        wanted = dot(spread, high) * 16.0 + dot(spread, low)
        place = 2 * lax.rem(row, cap)
        lanes = iota((chunk, 128), 1)
        first_item = jnp.sum(jnp.where(lanes == place, wanted, 0.0), axis=1, keepdims=True)
        second_item = jnp.sum(jnp.where(lanes == place + 1, wanted, 0.0), axis=1, keepdims=True)
        items = iota((chunk, table.shape[0]), 1).astype(F32)
        signs = jnp.where(items == first_item, 1.0, 0.0) - jnp.where(items == second_item, 1.0, 0.0)
        signs = signs.astype(BF16)
        group = lax.div(lax.rem(iota((chunk, quarter), 0), TILE), cap)
        total = jnp.zeros((chunk, quarter), F32)
        for g in range(4):
            term = dot(signs, table[:, g * quarter : (g + 1) * quarter])
            total = jnp.where(group == g, term, total)
        dsend[part * per : (part + 1) * per] = total.astype(BF16).reshape(per, TILE, quarter)

    def send_difference(i, carry):
        p = lax.rem(dp + i, ndp)
        rcopy(dsend.at[p], drecv.at[dp], dif_s, dif_r, (p, sq)).start()
        return carry

    lax.fori_loop(1, ndp, send_difference, 0)
    drecv[dp] = dsend[dp]
    for k in range(first, half):
        ring_step(k)
    y_forward(tok_copies)
    for copy in relays:
        copy.wait_recv()

    near = pl.ds(0, 2 * hd)
    far = pl.ds(2 * hd, 3 * hd)
    per_core = nx // CORES

    def weight_part(columns):
        def part(at, h):
            return wall.at[at, pl.ds(c * per_core, per_core), pl.ds(h * half, half), :, columns]

        return part

    def weight_relay(at, index, columns, send, recv):
        block = wall.at[at, pl.ds(c * per_core, per_core), :, :, columns]
        return rcopy(block, block, send.at[index], recv.at[index], sibling)

    near_copies = y_copies(weight_part(near), ws, wr)
    near_relays = [weight_relay(at, i, near, wrs, wrr) for i, at in enumerate((ym, yp, yo))]
    far_copies = y_copies(weight_part(far), vs, vr)
    far_relays = [weight_relay(at, i, far, vrs, vrr) for i, at in enumerate((ym, yp, yo))]

    def relay_start(copies, relayed):
        copies[2].wait_recv()
        relayed[0].start()
        copies[3].wait_recv()
        relayed[1].start()
        copies[4].wait_recv()
        copies[5].wait_recv()
        relayed[2].start()

    y_start(near_copies)

    length = jnp.sum(jnp.where(iota((1, ndp), 1) == dp, len_ref[...], 0), axis=1, keepdims=True)
    live_total = jnp.sum(len_ref[...], axis=1, keepdims=True).astype(F32)
    index = iota((rows, 1), 0)
    w_head = wall[y, :, :, :, 2 * hd : 5 * hd].reshape(width, 3 * hd)
    kv_copies = []

    def alive_of(block):
        return jnp.where(index + block * rows < length, 1.0, 0.0)

    def project(at, order):
        projected = dot(xn[at], w_head)
        proj[at] = projected
        activated = projected * jax.nn.sigmoid(projected)
        value, key = activated[:, :hd], activated[:, hd : 2 * hd] * alive_of(CORES * at + c)
        query = activated[:, 2 * hd :]
        kv[CORES * at + c, :, :hd] = value.astype(BF16)
        kv[CORES * at + c, :, hd:] = key.astype(BF16)
        copy = rcopy(kv.at[CORES * at + c], kv.at[CORES * at + c], ks.at[order], kr.at[order], sibling)
        copy.start()
        kv_copies.append(copy)
        vt[CORES * at + c] = value.T.astype(BF16)
        kt[CORES * at + c] = key.T.astype(BF16)
        qs[at] = query.astype(BF16)
        qt[at] = query.T.astype(BF16)

    project(y, 0)
    tok_copies[2].wait_recv()
    project(ym, 1)
    tok_copies[3].wait_recv()
    project(yp, 2)
    tok_copies[4].wait_recv()
    tok_copies[5].wait_recv()
    project(yo, 3)
    y_forward(near_copies)
    for copy in kv_copies:
        copy.wait_recv()
    for u in range(HEADS):
        block = CORES * u + other
        both = kv[block].astype(F32)
        vt[block] = both[:, :hd].T.astype(BF16)
        kt[block] = both[:, hd:].T.astype(BF16)

    def send_when(t, src, dst, send, recv):
        @pl.when(y != t)
        def _():
            rcopy(src, dst, send.at[t], recv.at[y], (dp, t * CORES + c)).start()

        @pl.when(y == t)
        def _():
            dst[...] = src[...]

    def wait_when(t, ref, send, recv):
        @pl.when(y != t)
        def _():
            rcopy(ref, ref, send.at[t], recv.at[t], (dp, t * CORES + c)).wait_recv()

    def done_when(t, ref, send, recv):
        @pl.when(y != t)
        def _():
            rcopy(ref, ref, send.at[t], recv.at[t], (dp, t * CORES + c)).wait_send()

    causal = jnp.where(iota((rows, rows), 0) <= iota((rows, rows), 1), 1.0, 0.0)
    before = c.astype(F32)
    for t in reversed(range(HEADS)):
        total = jnp.zeros((hd, rows), F32)
        for parity in range(2):
            for u in range(t + 1):
                block = CORES * u + (c if parity == 0 else other)
                scores = dot(kv[block, :, hd:], qt[t]) * scale
                sigma = jax.nn.sigmoid(scores)
                weights = scores * sigma
                change = (sigma + weights * (1.0 - sigma)) * (scale / history)
                weights = weights * (1.0 / history)
                if u == t:
                    mask = causal if parity == 0 else before
                    weights, change = weights * mask, change * mask
                weights = weights.astype(BF16)
                wst[pair(t, u, parity)] = weights
                slope[pair(t, u, parity)] = change
                total = total + dot(vt[block], weights)
        att_send[t] = total.T.astype(BF16)
        send_when(t, att_send.at[t], att_recv.at[y], as_, ar)

    relay_start(near_copies, near_relays)
    drop = rcopy(dsend.at[bulk], drecv.at[bulk], dif_s, dif_r, neighbour)
    drop.wait_recv()
    own_col = jnp.sum(
        jnp.where(iota((rows, ndp), 1) == lax.div(iota((rows, ndp), 0), cap), own_row, 0), axis=1, keepdims=True
    )
    received = drecv[...].reshape(ndp * TILE, quarter)
    source = own_col * TILE + lax.rem(index, cap)
    for g in range(4):
        pick = one_hot(iota((rows, ndp * TILE), 1) == source + g * cap)
        idiff[:, g * quarter : (g + 1) * quarter] = dot(pick, received).astype(BF16)
    for copy in near_relays:
        copy.wait_recv()
    for t in range(HEADS):
        gproj[:, t * hd : (t + 1) * hd] = dot(xn[y], wall[t, :, :, :, hd : 2 * hd].reshape(width, hd))
    shard = TILE // 2
    line, spot = iota((hw, width), 0), iota((hw, width), 1)
    origin = lax.div(line, shard) * TILE + lax.rem(line, shard)
    for side in range(2):
        select = one_hot(spot == origin + side * shard)
        for t in range(HEADS):
            begin = side * (width // 2) + t * hd
            wout[:, begin : begin + hd] = dot(select, wall[t, :, :, :, :hd].reshape(width, hd)).astype(BF16)

    eye = iota((rows, rows), 0) == iota((rows, rows), 1)
    teacher = jnp.sum(jnp.where(eye, teach_ref[...], 0.0), axis=1, keepdims=True)
    alive = alive_of(sq)
    projected = gproj[...]
    gate = (projected * jax.nn.sigmoid(projected)).astype(BF16).astype(F32)
    gain_mid = gmid_ref[...]
    for t in range(HEADS):
        wait_when(t, att_recv.at[t], as_, ar)
    y_start(far_copies)
    attended = jnp.concatenate([att_recv[t].astype(F32) for t in range(HEADS)], axis=1)
    normed_mid, factor_mid = normalize(attended)
    gated = (normed_mid * gain_mid * gate).astype(BF16)
    layer_out = (tok_ref[...].astype(F32) + dot(gated, wout[...])).astype(BF16).astype(F32)
    difference = idiff[...].astype(F32)
    errors = (jnp.sum(layer_out * difference, axis=1, keepdims=True) - teacher) * alive
    grad_out = (2.0 / live_total * errors * difference).astype(BF16)
    gout[...] = grad_out
    grad_gated = dot_nt(grad_out, wout[...])
    grad_normed = grad_gated * gain_mid * gate
    grad_attended = normalize_back(grad_normed, normed_mid, factor_mid).astype(BF16)
    for t in range(HEADS):
        da_send[t] = grad_attended[:, t * hd : (t + 1) * hd]
        send_when(t, da_send.at[t], da_recv.at[y], gs, gr)
    gpg[...] = (grad_gated * normed_mid * gain_mid * silu_slope(projected)).astype(BF16)

    lb0[sq] = jnp.broadcast_to(jnp.sum(errors * errors, axis=0, keepdims=True), (8, 128))
    loss_copies = []
    for d in range(1, nseq):
        device = (dp, lax.rem(sq + d, nseq))
        loss_copies.append(rcopy(lb0.at[sq], lb0.at[sq], l0s.at[d - 1], l0r.at[d - 1], device))
    for copy in loss_copies:
        copy.start()
    y_forward(far_copies)
    for t in range(HEADS):
        wait_when(t, da_recv.at[t], gs, gr)
    for t in range(HEADS):
        dat[t] = da_recv[t].astype(F32).T.astype(BF16)

    def backward(u, parity):
        block = CORES * u + (c if parity == 0 else other)
        grad_value = jnp.zeros((rows, hd), F32)
        grad_key = jnp.zeros((rows, hd), F32)
        for t in range(u, HEADS):
            n = pair(t, u, parity)
            grad_weights = dot(kv[block, :, :hd], dat[t])
            grad_scores = (grad_weights * slope[n]).astype(BF16)
            grad_value = grad_value + dot(wst[n], da_recv[t])
            grad_key = grad_key + dot(grad_scores, qs[t])
            term = dot(kt[block], grad_scores)
            if parity == 1 and u == 0:
                dqt[t] = term
            else:
                dqt[t] = dqt[t] + term
        return grad_value, grad_key

    part_copies = []
    for u in range(HEADS):
        grad_value, grad_key = backward(u, 1)
        dvk_send[u, :, :hd] = grad_value
        dvk_send[u, :, hd:] = grad_key
        copy = rcopy(dvk_send.at[u], dvk_recv.at[u], ps.at[u], pr.at[u], sibling)
        copy.start()
        part_copies.append(copy)
    relay_start(far_copies, far_relays)
    for copy in loss_copies:
        copy.wait_recv()
    lb1[x] = jnp.sum(lb0[...], axis=0)
    loss_x = []
    for d in range(1, nx):
        device = (lax.rem(x + d, nx) * NZ + z, sq)
        loss_x.append(rcopy(lb1.at[x], lb1.at[x], l1s.at[d - 1], l1r.at[d - 1], device))
    for copy in loss_x:
        copy.start()
    for u in range(HEADS):
        grad_value, grad_key = backward(u, 0)
        part_copies[u].wait_recv()
        keep = alive_of(CORES * u + c)
        grad_value = (grad_value + dvk_recv[u, :, :hd]) * keep
        grad_key = (grad_key + dvk_recv[u, :, hd:]) * keep
        grad_query = dqt[u].T
        gps[u, :, :hd] = (grad_value * silu_slope(proj[u, :, :hd])).astype(BF16)
        gps[u, :, hd : 2 * hd] = (grad_key * silu_slope(proj[u, :, hd : 2 * hd])).astype(BF16)
        gps[u, :, 2 * hd :] = (grad_query * silu_slope(proj[u, :, 2 * hd :])).astype(BF16)
        send_when(u, gps.at[u], gpr.at[y], fs, fr)

    for copy in loss_x:
        copy.wait_recv()
    lb2[z] = jnp.sum(lb1[...], axis=0)
    loss_z = []
    for d in range(1, NZ):
        device = (x * NZ + lax.rem(z + d, NZ), sq)
        loss_z.append(rcopy(lb2.at[z], lb2.at[z], l2s.at[d - 1], l2r.at[d - 1], device))
    for copy in loss_z:
        copy.start()

    for copy in far_relays:
        copy.wait_recv()
    grad_in = jnp.zeros((rows, width), F32)
    for t in range(HEADS):
        grad_in = grad_in + dot_nt(
            gpg[:, t * hd : (t + 1) * hd], wall[t, :, :, :, hd : 2 * hd].reshape(width, hd)
        )
    for t in range(HEADS):
        wait_when(t, gpr.at[t], fs, fr)
        grad_in = grad_in + dot_nt(gpr[t], wall[t, :, :, :, 2 * hd :].reshape(width, 3 * hd))
    normed_raw, factor_in = normalize(tok_ref[...].astype(F32))
    grad_norm = normalize_back(grad_in * gin_ref[...], normed_raw, factor_in)
    out_ref[...] = (gout[...].astype(F32) + grad_norm).astype(BF16)

    for copy in loss_z:
        copy.wait_recv()
    loss_ref[...] = jnp.sum(lb2[...], axis=0) / live_total

    for copy in x_copies + z_copies + relays + tok_copies + near_copies + near_relays + far_copies + far_relays:
        copy.wait_send()
    for copy in kv_copies + part_copies + loss_copies + loss_x + loss_z:
        copy.wait_send()
    request_bulk.wait_send()
    drop.wait_send()
    for t in range(HEADS):
        done_when(t, att_send.at[t], as_, ar)
        done_when(t, da_send.at[t], gs, gr)
        done_when(t, gps.at[t], fs, fr)


def on_device(
    tokens, teacher, cand_items, owner_map, lengths, w_proj, w_out, gain_in, gain_mid, item_table
):
    rows, width = tokens.shape
    ndp = lax.axis_size("dp")
    nx = ndp // NZ
    hw = gain_mid.shape[0]
    hd = hw // HEADS
    blocks = HEADS * CORES
    pairs = HEADS * (HEADS + 1)
    half = NZ // 2
    quarter = width // 4
    w_out_tile = jnp.concatenate([w_out[:, : width // 2], w_out[:, width // 2 :]], axis=0)

    vmem = pltpu.VMEM
    dma = pltpu.SemaphoreType.DMA
    scratch = [
        vmem((HEADS, nx, NZ, TILE, 5 * hd), BF16),
        vmem((HEADS, rows, width), BF16),
        vmem(item_table.shape, BF16),
        vmem((ndp, 1, 128), F32),
        vmem((ndp, 1, 128), F32),
        vmem((ndp, 128), F32),
        vmem((ndp, TILE, quarter), BF16),
        vmem((ndp, TILE, quarter), BF16),
        vmem((rows, width), BF16),
        vmem((HEADS, rows, 3 * hd), F32),
        vmem((blocks, rows, 2 * hd), BF16),
        vmem((blocks, hd, rows), BF16),
        vmem((blocks, hd, rows), BF16),
        vmem((HEADS, rows, hd), BF16),
        vmem((HEADS, hd, rows), BF16),
        vmem((pairs, rows, rows), BF16),
        vmem((pairs, rows, rows), F32),
        vmem((HEADS, rows, hd), BF16),
        vmem((HEADS, rows, hd), BF16),
        vmem((rows, hw), F32),
        vmem((hw, width), BF16),
        vmem((rows, width), BF16),
        vmem((rows, hw), BF16),
        vmem((HEADS, rows, hd), BF16),
        vmem((HEADS, rows, hd), BF16),
        vmem((HEADS, hd, rows), BF16),
        vmem((HEADS, rows, 2 * hd), F32),
        vmem((HEADS, rows, 2 * hd), F32),
        vmem((HEADS, hd, rows), F32),
        vmem((HEADS, rows, 3 * hd), BF16),
        vmem((HEADS, rows, 3 * hd), BF16),
        vmem((blocks, 8, 128), F32),
        vmem((nx, 8, 128), F32),
        vmem((NZ, 8, 128), F32),
        dma((6,)),
        dma((nx,)), dma((nx,)),
        dma((half,)), dma((half,)),
        dma((half,)), dma((half,)),
        dma((6,)), dma((6,)),
        dma, dma,
        dma, dma,
        dma((6,)), dma((6,)), dma((3,)), dma((3,)),
        dma((6,)), dma((6,)), dma((3,)), dma((3,)),
        dma((HEADS,)), dma((HEADS,)),
        dma((HEADS,)), dma((HEADS,)),
        dma((HEADS,)), dma((HEADS,)),
        dma((HEADS,)), dma((HEADS,)),
        dma((HEADS,)), dma((HEADS,)),
        dma((blocks,)), dma((blocks,)), dma((nx,)), dma((nx,)), dma((NZ,)), dma((NZ,)),
    ]
    whole = pl.BlockSpec(memory_space=pltpu.VMEM)
    anywhere = pl.BlockSpec(memory_space=pl.ANY)
    grads, loss = pl.pallas_call(
        kernel,
        out_shape=(jax.ShapeDtypeStruct(tokens.shape, BF16), jax.ShapeDtypeStruct((8, 128), F32)),
        in_specs=[whole] * 5 + [anywhere, anywhere, whole, whole, anywhere],
        out_specs=(whole, whole),
        scratch_shapes=scratch,
        compiler_params=pltpu.CompilerParams(
            collective_id=0, has_side_effects=True, vmem_limit_bytes=56 * 1024 * 1024
        ),
    )(
        tokens,
        teacher.reshape(1, rows),
        cand_items.T,
        owner_map.reshape(1, ndp),
        lengths.reshape(1, ndp),
        w_proj,
        w_out_tile,
        gain_in.reshape(1, width),
        gain_mid.reshape(1, hw),
        item_table,
    )
    return (grads, loss[0, 0])


def solution(mesh):
    in_specs = (
        P(("dp", "seq"), None),
        P(("dp", "seq")),
        P(("dp", "seq"), None),
        P(("dp", "seq")),
        P(),
        P("dp", None),
        P("dp", None),
        P(),
        P(),
        P("dp", None),
    )
    out_specs = (P(("dp", "seq"), None), P())
    return jax.shard_map(
        on_device, mesh=mesh, in_specs=in_specs, out_specs=out_specs, check_vma=False
    )
```

time: 718 us -> 131 us (0.18)
  waiting for transfers between devices: 311 us -> 0 us
  Pallas kernels: 0 us -> 125 us
  blocking collectives: 114 us -> 0 us
  matrix products: 72.5 us -> 0 us
  local copies, waits for them, and re-layouts: 56.7 us -> 3.78 us
  other arithmetic: 51.5 us -> 0.61 us
  starting transfers between devices: 50 us -> 0 us
  loops' own time: 41.2 us -> 0 us
  between operations: 19 us -> 0.64 us
    all_gather x6 -> x0, waiting for transfers between devices: 251 us -> none  [the longest x1 143 us: on_device(): lax.all_gather(w_proj, 'dp', axis=0, tiled=True)]
    pallas_call x0 -> x1, Pallas kernels: none -> 125 us  [on_device(): pl.pallas_call(kernel, out_shape=(jax.ShapeDtypeStruct(tokens.shape, BF16...]
    psum x1 -> x0, blocking collectives: 114 us -> none  [on_device(): loss = lax.psum(loss_part, ('dp', 'seq')) / live_total]
    dot_general x31 -> x0, matrix products: 72.5 us -> none  [the longest x9 14.8 us: tile_scores(): jnp.einsum('qhd,khd->hqk', split_heads(query_rows, head_count), split_hea...]
    all_to_all x6 -> x0, waiting for transfers between devices: 57.8 us -> none  [the longest x1 20.5 us: on_device(): lax.all_to_all(grad_rows, 'dp', split_axis=0, concat_axis=0, tiled=True)]
    all_to_all x6 -> x0, starting transfers between devices: 49.6 us -> none  [the longest x1 14.2 us: on_device(): lax.all_to_all(bucket(alive_rows).astype(jnp.bfloat16), 'dp', split_axis=...]
    another operation x19 -> x0, loops' own time: 41.2 us -> none  [the longest x2 40 us: fold_pieces(): return lax.fori_loop(0, count, step, initial)]
    dynamic_slice x17 -> x0, local copies, waits for them, and re-layouts: 23.4 us -> none  [the longest x16 22.8 us: step(): lax.dynamic_slice_in_dim(array, offset, row_count, 0)]
  transfers between devices with their start and end apart: 12 -> 0, of which waited for: 8 -> 0; matrix products, arithmetic and copies ran while one was open for 19% -> 0% of each run, Pallas kernels for 0% -> 0%
where the time goes in v1:
time: 131 us; the launch traced here: 130 us
  Pallas kernels  125 us (95%)
  local copies, waits for them, and re-layouts  3.78 us (3%)
    pallas_call x1, Pallas kernels, on_device(): pl.pallas_call(kernel, out_shape=(jax.ShapeDtypeStruct(tokens.shape, BF16...  125 us

profile of v1, /device:TPU:25, one launch (start us, length us, event | category | flops | bytes accessed | tf_op | source)
XLA Modules:
  0.0 130.5 jit_solution(13420411436112150535)
XLA Ops:
  0.6 0.7 fusion
  1.3 0.6 pad_maximum_fusion.wo_ref
  2.0 125.4 %shard_map.113 = (bf16[256,1024]{1,0:T(8,128)(2,1)}, f32[8,128]{1,0:T(8,128)}) custom-call(bf16[256,1024]{1,0:T(8,128)(2,1)} %tok_ref.1, f32[1,256]{1,0:T(1,128)} %bitcast.10, s32[2,256]{1,0:T(2,128)} %bitcast.8, s32[1,64]{1,0:T(1,128)} %bitcast.11, s32[1,64]{1,0:T(1,128)} %bitcast.12, bf16[16,2048]{1,0:T(8,128)(2,1)} %wp_ref.1, ...), custom_call_target="tpu_custom_call" | custom-call | tf_op jit(solution)/shard_map/pallas_call | solution.py:581
  127.4 1.2 slice.11
  128.6 1.9 %copy.13 = bf16[256,1024]{1,0:T(8,128)(2,1)} copy(bf16[256,1024]{1,0:T(8,128)(2,1)} %get-tuple-element.10) | data formatting | bytes 1048576

commit v2 on v1

--- a/solution.py
+++ b/solution.py
@@ -59,18 +59,19 @@
 
 
 def kernel(
-    tok_ref, teach_ref, cand_ref, own_ref, len_ref, wp_ref, wo_ref, gin_ref, gmid_ref, table_hbm,
+    tok_hbm, teach_hbm, cand_hbm, own_hbm, len_hbm, wp_ref, wo_hbm, gin_hbm, gmid_hbm, table_hbm,
     out_ref, loss_ref,
-    wall, xn, table, req_send, req_recv, rq, dsend, drecv, idiff, proj, kv, kt, vt, qs, qt, wst, slope,
+    tok_ref, teach_ref, cand_ref, own_ref, len_ref, wo_ref, gin_ref, gmid_ref,
+    wall, xn, table, req_send, req_mid, req_recv, rq, dsend, dmid, drecv, idiff, proj, kv, kt, vt, qs, qt, wst, slope,
     att_send, att_recv, gproj, wout, gout, gpg, da_send, da_recv, dat, dvk_send, dvk_recv, dqt,
-    gps, gpr, lb0, lb1, lb2,
-    lsem, xs, xr, zs, zr, rs, rr, ts, tr, req_s, req_r, dif_s, dif_r,
-    ws, wr, wrs, wrr, vs, vr, vrs, vrr, ks, kr, as_, ar, gs, gr, ps, pr, fs, fr, l0s, l0r, l1s, l1r, l2s, l2r,
+    gps, gpr, lby, lbc, lbx, lbz,
+    lsem, isem, xs, xr, zs, zr, rs, rr, ts, tr, qxs, qxr, qzs, qzr, dxs, dxr, dzs, dzr,
+    ws, wr, wrs, wrr, vs, vr, vrs, vrr, ks, kr, as_, ar, gs, gr, ps, pr, fs, fr, lys, lyr, lcs, lcr, lxs, lxr, lzs, lzr,
 ):
     rows, width = tok_ref.shape
     hd = kv.shape[2] // 2
-    ndp = req_send.shape[0]
-    nx = ndp // NZ
+    nx = req_send.shape[0]
+    ndp = nx * NZ
     nseq = HEADS * CORES
     half = NZ // 2
     cap = rows // ndp
@@ -94,34 +95,40 @@
             src_ref=src, dst_ref=dst, send_sem=send, recv_sem=recv, device_id=device, device_id_type=MESH
         )
 
+    def beside_x(d):
+        return (lax.rem(x + d, nx) * NZ + z, sq)
+
+    def beside_z(d):
+        return (x * NZ + lax.rem(z + d, NZ), sq)
+
+    def beside_y(d):
+        return (dp, lax.rem(y + d, HEADS) * CORES + c)
+
     barrier = pltpu.get_barrier_semaphore()
-
-    def greet(i, carry):
-        pl.semaphore_signal(barrier, inc=1, device_id=(lax.rem(dp + i, ndp), sq), device_id_type=MESH)
-        return carry
-
-    lax.fori_loop(1, ndp, greet, 0)
-    for d in range(1, nseq):
-        pl.semaphore_signal(barrier, inc=1, device_id=(dp, lax.rem(sq + d, nseq)), device_id_type=MESH)
+    partners = [sibling] + [beside_y(d) for d in range(1, HEADS)]
+    partners += [beside_x(d) for d in range(1, nx)] + [beside_z(d) for d in range(1, NZ)]
+    for device in partners:
+        pl.semaphore_signal(barrier, inc=1, device_id=device, device_id_type=MESH)
 
     hw = HEADS * hd
-    pieces = [
-        (wo_ref, 0, 0),
-        (wp_ref, 0, hd),
-        (wp_ref, hw, 2 * hd),
-        (wp_ref, 3 * hw, 3 * hd),
-        (wp_ref, 2 * hw, 4 * hd),
+    arguments = [
+        (tok_hbm, tok_ref), (gin_hbm, gin_ref), (own_hbm, own_ref), (cand_hbm, cand_ref),
+        (wo_hbm, wo_ref), (len_hbm, len_ref), (teach_hbm, teach_ref), (gmid_hbm, gmid_ref),
     ]
+    inputs = [pltpu.make_async_copy(src, dst, isem.at[i]) for i, (src, dst) in enumerate(arguments)]
+    pieces = [(0, hd), (hw, 2 * hd), (3 * hw, 3 * hd), (2 * hw, 4 * hd)]
     local = []
-    for i, (src, start, to) in enumerate(pieces):
+    for i, (start, to) in enumerate(pieces):
         begin = pl.multiple_of(start + y * hd, hd)
         local.append(
-            pltpu.make_async_copy(src.at[:, pl.ds(begin, hd)], wall.at[y, x, z, :, pl.ds(to, hd)], lsem.at[i])
+            pltpu.make_async_copy(wp_ref.at[:, pl.ds(begin, hd)], wall.at[y, x, z, :, pl.ds(to, hd)], lsem.at[i])
         )
-    table_copy = pltpu.make_async_copy(table_hbm, table, lsem.at[5])
-    for copy in local:
+    table_copy = pltpu.make_async_copy(table_hbm, table, lsem.at[4])
+    for copy in inputs + local:
         copy.start()
     table_copy.start()
+    for copy in inputs:
+        copy.wait()
 
     tokens = tok_ref[...].astype(F32)
     normed_raw, factor_in = normalize(tokens)
@@ -137,16 +144,17 @@
     high, low = small_parts(jnp.where(inside, both, 0))
     requests = dot_nt(to_owner, high) * 16.0 + dot_nt(to_owner, low)
     for p in range(ndp):
-        req_send[p] = requests[p : p + 1, :]
+        req_send[p // NZ, p % NZ] = requests[p : p + 1, :]
+    sides = [wo_ref[:, pl.ds(pl.multiple_of(i * (width // 2) + y * hd, hd), hd)].astype(F32) for i in range(2)]
+    wall[y, x, z, :, :hd] = jnp.concatenate(sides, axis=0).astype(BF16)
 
     for copy in local:
         copy.wait()
-    pl.semaphore_wait(barrier, ndp - 1 + nseq - 1)
+    pl.semaphore_wait(barrier, len(partners))
 
     x_copies = []
     for d in range(1, nx):
-        device = (lax.rem(x + d, nx) * NZ + z, sq)
-        copy = rcopy(wall.at[y, x, z], wall.at[y, x, z], xs.at[d - 1], xr.at[d - 1], device)
+        copy = rcopy(wall.at[y, x, z], wall.at[y, x, z], xs.at[d - 1], xr.at[d - 1], beside_x(d))
         copy.start()
         x_copies.append(copy)
 
@@ -171,15 +179,14 @@
         copies[5].start()
 
     tok_copies = y_copies(lambda at, h: xn.at[at, pl.ds(h * (rows // 2), rows // 2), :], ts, tr)
-    y_start(tok_copies)
-
-    def send_request(i, carry):
-        p = lax.rem(dp + i, ndp)
-        rcopy(req_send.at[p], req_recv.at[dp], req_s, req_r, (p, sq)).start()
-        return carry
-
-    lax.fori_loop(1, ndp, send_request, 0)
-    req_recv[dp] = req_send[dp]
+
+    request_x = []
+    for d in range(1, nx):
+        block = req_send.at[lax.rem(x + d, nx)]
+        request_x.append(rcopy(block, req_mid.at[x], qxs.at[d - 1], qxr.at[d - 1], beside_x(d)))
+    for copy in request_x:
+        copy.start()
+    req_mid[x] = req_send[x]
 
     def at_z(distance):
         return lax.rem(z - way * distance + NZ, NZ)
@@ -202,23 +209,32 @@
     for copy in x_copies:
         copy.wait_recv()
     z_copies[0].start()
+    y_start(tok_copies)
+    for copy in request_x:
+        copy.wait_recv()
+    request_z = []
+    for d in range(1, NZ):
+        block = req_mid.at[:, lax.rem(z + d, NZ)]
+        request_z.append(rcopy(block, req_recv.at[:, z], qzs.at[d - 1], qzr.at[d - 1], beside_z(d)))
+    for copy in request_z:
+        copy.start()
+    req_recv[:, z] = req_mid[:, z]
     first = min(2, half)
     for k in range(first):
         ring_step(k)
 
-    bulk = pl.ds(0, ndp - 1)
-    neighbour = (lax.rem(dp + 1, ndp), sq)
-    request_bulk = rcopy(req_send.at[bulk], req_recv.at[bulk], req_s, req_r, neighbour)
-    request_bulk.wait_recv()
+    for copy in request_z:
+        copy.wait_recv()
     for p in range(ndp):
-        rq[p : p + 1, :] = req_recv[p]
+        rq[p : p + 1, :] = req_recv[p // NZ, p % NZ]
     table_copy.wait()
     high, low = small_parts(rq[...])
-    chunk = ndp * TILE // 4
-    per = chunk // TILE
-    for part in range(4):
+    chunk = NZ * TILE
+    diff_x = []
+    for d in range(nx):
+        side = lax.rem(x + d + 1, nx)
         row = iota((chunk, 128), 0)
-        spread = one_hot(lax.div(iota((chunk, ndp), 0), TILE) + part * per == iota((chunk, ndp), 1))
+        spread = one_hot(lax.div(iota((chunk, ndp), 0), TILE) + side * NZ == iota((chunk, ndp), 1))
         wanted = dot(spread, high) * 16.0 + dot(spread, low)
         place = 2 * lax.rem(row, cap)
         lanes = iota((chunk, 128), 1)
@@ -232,18 +248,31 @@
         for g in range(4):
             term = dot(signs, table[:, g * quarter : (g + 1) * quarter])
             total = jnp.where(group == g, term, total)
-        dsend[part * per : (part + 1) * per] = total.astype(BF16).reshape(per, TILE, quarter)
-
-    def send_difference(i, carry):
-        p = lax.rem(dp + i, ndp)
-        rcopy(dsend.at[p], drecv.at[dp], dif_s, dif_r, (p, sq)).start()
-        return carry
-
-    lax.fori_loop(1, ndp, send_difference, 0)
-    drecv[dp] = dsend[dp]
-    for k in range(first, half):
+        total = total.astype(BF16).reshape(NZ, TILE, quarter)
+        if d + 1 < nx:
+            dsend[side] = total
+            diff_x.append(rcopy(dsend.at[side], dmid.at[x], dxs.at[d], dxr.at[d], beside_x(d + 1)))
+            diff_x[d].start()
+        else:
+            dmid[x] = total
+        if first + d < half:
+            ring_step(first + d)
+    y_forward(tok_copies)
+    first = first + nx
+    if first < half:
+        ring_step(first)
+
+    for copy in diff_x:
+        copy.wait_recv()
+    diff_z = []
+    for d in range(1, NZ):
+        block = dmid.at[:, lax.rem(z + d, NZ)]
+        diff_z.append(rcopy(block, drecv.at[:, z], dzs.at[d - 1], dzr.at[d - 1], beside_z(d)))
+    for copy in diff_z:
+        copy.start()
+    drecv[:, z] = dmid[:, z]
+    for k in range(first + 1, half):
         ring_step(k)
-    y_forward(tok_copies)
     for copy in relays:
         copy.wait_recv()
 
@@ -311,6 +340,7 @@
     tok_copies[5].wait_recv()
     project(yo, 3)
     y_forward(near_copies)
+    y_start(far_copies)
     for copy in kv_copies:
         copy.wait_recv()
     for u in range(HEADS):
@@ -361,8 +391,9 @@
         send_when(t, att_send.at[t], att_recv.at[y], as_, ar)
 
     relay_start(near_copies, near_relays)
-    drop = rcopy(dsend.at[bulk], drecv.at[bulk], dif_s, dif_r, neighbour)
-    drop.wait_recv()
+    y_forward(far_copies)
+    for copy in diff_z:
+        copy.wait_recv()
     own_col = jnp.sum(
         jnp.where(iota((rows, ndp), 1) == lax.div(iota((rows, ndp), 0), cap), own_row, 0), axis=1, keepdims=True
     )
@@ -392,7 +423,6 @@
     gain_mid = gmid_ref[...]
     for t in range(HEADS):
         wait_when(t, att_recv.at[t], as_, ar)
-    y_start(far_copies)
     attended = jnp.concatenate([att_recv[t].astype(F32) for t in range(HEADS)], axis=1)
     normed_mid, factor_mid = normalize(attended)
     gated = (normed_mid * gain_mid * gate).astype(BF16)
@@ -409,14 +439,17 @@
         send_when(t, da_send.at[t], da_recv.at[y], gs, gr)
     gpg[...] = (grad_gated * normed_mid * gain_mid * silu_slope(projected)).astype(BF16)
 
-    lb0[sq] = jnp.broadcast_to(jnp.sum(errors * errors, axis=0, keepdims=True), (8, 128))
-    loss_copies = []
-    for d in range(1, nseq):
-        device = (dp, lax.rem(sq + d, nseq))
-        loss_copies.append(rcopy(lb0.at[sq], lb0.at[sq], l0s.at[d - 1], l0r.at[d - 1], device))
-    for copy in loss_copies:
-        copy.start()
-    y_forward(far_copies)
+    def loss_send(buffer, place, send, recv, devices):
+        copies = [
+            rcopy(buffer.at[place], buffer.at[place], send.at[i], recv.at[i], device)
+            for i, device in enumerate(devices)
+        ]
+        for copy in copies:
+            copy.start()
+        return copies
+
+    lby[y] = jnp.broadcast_to(jnp.sum(errors * errors, axis=0, keepdims=True), (8, 128))
+    loss_y = loss_send(lby, y, lys, lyr, [beside_y(d) for d in range(1, HEADS)])
     for t in range(HEADS):
         wait_when(t, da_recv.at[t], gs, gr)
     for t in range(HEADS):
@@ -448,15 +481,10 @@
         copy.start()
         part_copies.append(copy)
     relay_start(far_copies, far_relays)
-    for copy in loss_copies:
-        copy.wait_recv()
-    lb1[x] = jnp.sum(lb0[...], axis=0)
-    loss_x = []
-    for d in range(1, nx):
-        device = (lax.rem(x + d, nx) * NZ + z, sq)
-        loss_x.append(rcopy(lb1.at[x], lb1.at[x], l1s.at[d - 1], l1r.at[d - 1], device))
-    for copy in loss_x:
-        copy.start()
+    for copy in loss_y:
+        copy.wait_recv()
+    lbc[c] = jnp.sum(lby[...], axis=0)
+    loss_c = loss_send(lbc, c, lcs, lcr, [sibling])
     for u in range(HEADS):
         grad_value, grad_key = backward(u, 0)
         part_copies[u].wait_recv()
@@ -468,16 +496,15 @@
         gps[u, :, hd : 2 * hd] = (grad_key * silu_slope(proj[u, :, hd : 2 * hd])).astype(BF16)
         gps[u, :, 2 * hd :] = (grad_query * silu_slope(proj[u, :, 2 * hd :])).astype(BF16)
         send_when(u, gps.at[u], gpr.at[y], fs, fr)
+        if u == 0:
+            loss_c[0].wait_recv()
+            lbx[x] = jnp.sum(lbc[...], axis=0)
+            loss_x = loss_send(lbx, x, lxs, lxr, [beside_x(d) for d in range(1, nx)])
 
     for copy in loss_x:
         copy.wait_recv()
-    lb2[z] = jnp.sum(lb1[...], axis=0)
-    loss_z = []
-    for d in range(1, NZ):
-        device = (x * NZ + lax.rem(z + d, NZ), sq)
-        loss_z.append(rcopy(lb2.at[z], lb2.at[z], l2s.at[d - 1], l2r.at[d - 1], device))
-    for copy in loss_z:
-        copy.start()
+    lbz[z] = jnp.sum(lbx[...], axis=0)
+    loss_z = loss_send(lbz, z, lzs, lzr, [beside_z(d) for d in range(1, NZ)])
 
     for copy in far_relays:
         copy.wait_recv()
@@ -495,14 +522,14 @@
 
     for copy in loss_z:
         copy.wait_recv()
-    loss_ref[...] = jnp.sum(lb2[...], axis=0) / live_total
+    loss_ref[...] = jnp.sum(lbz[...], axis=0)[0:1, 0:1] / live_total
 
     for copy in x_copies + z_copies + relays + tok_copies + near_copies + near_relays + far_copies + far_relays:
         copy.wait_send()
-    for copy in kv_copies + part_copies + loss_copies + loss_x + loss_z:
+    for copy in kv_copies + part_copies + loss_y + loss_c + loss_x + loss_z:
         copy.wait_send()
-    request_bulk.wait_send()
-    drop.wait_send()
+    for copy in request_x + request_z + diff_x + diff_z:
+        copy.wait_send()
     for t in range(HEADS):
         done_when(t, att_send.at[t], as_, ar)
         done_when(t, da_send.at[t], gs, gr)
@@ -521,19 +548,28 @@
     pairs = HEADS * (HEADS + 1)
     half = NZ // 2
     quarter = width // 4
-    w_out_tile = jnp.concatenate([w_out[:, : width // 2], w_out[:, width // 2 :]], axis=0)
 
     vmem = pltpu.VMEM
     dma = pltpu.SemaphoreType.DMA
     scratch = [
+        vmem((rows, width), BF16),
+        vmem((1, rows), F32),
+        vmem((2, rows), jnp.int32),
+        vmem((1, ndp), jnp.int32),
+        vmem((1, ndp), jnp.int32),
+        vmem(w_out.shape, BF16),
+        vmem((1, width), F32),
+        vmem((1, hw), F32),
         vmem((HEADS, nx, NZ, TILE, 5 * hd), BF16),
         vmem((HEADS, rows, width), BF16),
         vmem(item_table.shape, BF16),
-        vmem((ndp, 1, 128), F32),
-        vmem((ndp, 1, 128), F32),
+        vmem((nx, NZ, 1, 128), F32),
+        vmem((nx, NZ, 1, 128), F32),
+        vmem((nx, NZ, 1, 128), F32),
         vmem((ndp, 128), F32),
-        vmem((ndp, TILE, quarter), BF16),
-        vmem((ndp, TILE, quarter), BF16),
+        vmem((nx, NZ, TILE, quarter), BF16),
+        vmem((nx, NZ, TILE, quarter), BF16),
+        vmem((nx, NZ, TILE, quarter), BF16),
         vmem((rows, width), BF16),
         vmem((HEADS, rows, 3 * hd), F32),
         vmem((blocks, rows, 2 * hd), BF16),
@@ -557,16 +593,18 @@
         vmem((HEADS, hd, rows), F32),
         vmem((HEADS, rows, 3 * hd), BF16),
         vmem((HEADS, rows, 3 * hd), BF16),
-        vmem((blocks, 8, 128), F32),
+        vmem((HEADS, 8, 128), F32),
+        vmem((CORES, 8, 128), F32),
         vmem((nx, 8, 128), F32),
         vmem((NZ, 8, 128), F32),
-        dma((6,)),
+        dma((5,)),
+        dma((8,)),
         dma((nx,)), dma((nx,)),
         dma((half,)), dma((half,)),
         dma((half,)), dma((half,)),
         dma((6,)), dma((6,)),
-        dma, dma,
-        dma, dma,
+        dma((nx,)), dma((nx,)), dma((NZ,)), dma((NZ,)),
+        dma((nx,)), dma((nx,)), dma((NZ,)), dma((NZ,)),
         dma((6,)), dma((6,)), dma((3,)), dma((3,)),
         dma((6,)), dma((6,)), dma((3,)), dma((3,)),
         dma((HEADS,)), dma((HEADS,)),
@@ -574,14 +612,14 @@
         dma((HEADS,)), dma((HEADS,)),
         dma((HEADS,)), dma((HEADS,)),
         dma((HEADS,)), dma((HEADS,)),
-        dma((blocks,)), dma((blocks,)), dma((nx,)), dma((nx,)), dma((NZ,)), dma((NZ,)),
+        dma((HEADS,)), dma((HEADS,)), dma((1,)), dma((1,)), dma((nx,)), dma((nx,)), dma((NZ,)), dma((NZ,)),
     ]
     whole = pl.BlockSpec(memory_space=pltpu.VMEM)
     anywhere = pl.BlockSpec(memory_space=pl.ANY)
     grads, loss = pl.pallas_call(
         kernel,
-        out_shape=(jax.ShapeDtypeStruct(tokens.shape, BF16), jax.ShapeDtypeStruct((8, 128), F32)),
-        in_specs=[whole] * 5 + [anywhere, anywhere, whole, whole, anywhere],
+        out_shape=(jax.ShapeDtypeStruct(tokens.shape, BF16), jax.ShapeDtypeStruct((1, 1), F32)),
+        in_specs=[anywhere] * 10,
         out_specs=(whole, whole),
         scratch_shapes=scratch,
         compiler_params=pltpu.CompilerParams(
@@ -594,7 +632,7 @@
         owner_map.reshape(1, ndp),
         lengths.reshape(1, ndp),
         w_proj,
-        w_out_tile,
+        w_out,
         gain_in.reshape(1, width),
         gain_mid.reshape(1, hw),
         item_table,

time: 131 us -> 110 us (0.84)
  Pallas kernels: 125 us -> 104 us
  local copies, waits for them, and re-layouts: 3.78 us -> 1.87 us
  between operations: 0.64 us -> 2.34 us
    pallas_call x1, Pallas kernels: 125 us -> 104 us  [on_device(): pl.pallas_call(kernel, out_shape=(jax.ShapeDtypeStruct(tokens.shape, BF16...]
    slice x2 -> x0, local copies, waits for them, and re-layouts: 1.91 us -> none  [the longest x1 1.19 us: on_device(): return (grads, loss[0, 0])]
where the time goes in v2:
time: 110 us; the launch traced here: 108 us
  Pallas kernels  104 us (95%)
  between operations  2.34 us (2%)
  local copies, waits for them, and re-layouts  1.87 us (2%)
    pallas_call x1, Pallas kernels, on_device(): pl.pallas_call(kernel, out_shape=(jax.ShapeDtypeStruct(tokens.shape, BF16...  104 us

profile of v2, /device:TPU:25, one launch (start us, length us, event | category | flops | bytes accessed | tf_op | source)
XLA Modules:
  0.0 108.3 jit_solution(17254279662841074204)
XLA Ops:
  0.6 104.1 %shard_map.113 = (bf16[256,1024]{1,0:T(8,128)(2,1)}, f32[1,1]{1,0:T(1,128)}) custom-call(bf16[256,1024]{1,0:T(8,128)(2,1)} %tok_hbm.1, f32[1,256]{1,0:T(1,128)} %bitcast.10, s32[2,256]{1,0:T(2,128)} %bitcast.8, s32[1,64]{1,0:T(1,128)} %bitcast.11, s32[1,64]{1,0:T(1,128)} %bitcast.12, bf16[16,2048]{1,0:T(8,128)(2,1)} %wp_ref.1, bf16[8,1024]{1,0:T(8,128)(2,1)} %wo_hbm.1, ...), custom_call_target="tpu_custom_call" | custom-call | tf_op jit(solution)/shard_map/pallas_call | solution.py:619
  104.7 1.9 %copy.14 = bf16[256,1024]{1,0:T(8,128)(2,1)} copy(bf16[256,1024]{1,0:T(8,128)(2,1)} %get-tuple-element.8) | data formatting | bytes 1048576

commit v3 on v2

--- a/solution.py
+++ b/solution.py
@@ -54,18 +54,14 @@
     return (whole >> 4).astype(F32).astype(BF16), (whole & 15).astype(F32).astype(BF16)
 
 
-def pair(t, u, parity):
-    return t * (t + 1) + 2 * u + parity
-
-
 def kernel(
     tok_hbm, teach_hbm, cand_hbm, own_hbm, len_hbm, wp_ref, wo_hbm, gin_hbm, gmid_hbm, table_hbm,
     out_ref, loss_ref,
     tok_ref, teach_ref, cand_ref, own_ref, len_ref, wo_ref, gin_ref, gmid_ref,
     wall, xn, table, req_send, req_mid, req_recv, rq, dsend, dmid, drecv, idiff, proj, kv, kt, vt, qs, qt, wst, slope,
-    att_send, att_recv, gproj, wout, gout, gpg, da_send, da_recv, dat, dvk_send, dvk_recv, dqt,
+    att_send, att_recv, gproj, wout, gout, gpg, da_send, da_recv, dat, dvk_send, dvk_recv, dst,
     gps, gpr, lby, lbc, lbx, lbz,
-    lsem, isem, xs, xr, zs, zr, rs, rr, ts, tr, qxs, qxr, qzs, qzr, dxs, dxr, dzs, dzr,
+    lsem, isem, xs, xr, zs, zr, rs, rr, ts, tr, qxs, qxr, qzs, qzr, dxs, dxr, dzs, dzr, ezs, ezr,
     ws, wr, wrs, wrr, vs, vr, vrs, vrr, ks, kr, as_, ar, gs, gr, ps, pr, fs, fr, lys, lyr, lcs, lcr, lxs, lxr, lzs, lzr,
 ):
     rows, width = tok_ref.shape
@@ -152,12 +148,6 @@
         copy.wait()
     pl.semaphore_wait(barrier, len(partners))
 
-    x_copies = []
-    for d in range(1, nx):
-        copy = rcopy(wall.at[y, x, z], wall.at[y, x, z], xs.at[d - 1], xr.at[d - 1], beside_x(d))
-        copy.start()
-        x_copies.append(copy)
-
     def y_copies(part, send, recv):
         return [
             rcopy(part(y, 0), part(y, 0), send.at[0], recv.at[0], up),
@@ -187,6 +177,22 @@
     for copy in request_x:
         copy.start()
     req_mid[x] = req_send[x]
+    x_copies = []
+    for d in range(1, nx):
+        copy = rcopy(wall.at[y, x, z], wall.at[y, x, z], xs.at[d - 1], xr.at[d - 1], beside_x(d))
+        copy.start()
+        x_copies.append(copy)
+    y_start(tok_copies)
+
+    for copy in request_x:
+        copy.wait_recv()
+    request_z = []
+    for d in range(1, NZ):
+        block = req_mid.at[:, lax.rem(z + d, NZ)]
+        request_z.append(rcopy(block, req_recv.at[:, z], qzs.at[d - 1], qzr.at[d - 1], beside_z(d)))
+    for copy in request_z:
+        copy.start()
+    req_recv[:, z] = req_mid[:, z]
 
     def at_z(distance):
         return lax.rem(z - way * distance + NZ, NZ)
@@ -209,19 +215,6 @@
     for copy in x_copies:
         copy.wait_recv()
     z_copies[0].start()
-    y_start(tok_copies)
-    for copy in request_x:
-        copy.wait_recv()
-    request_z = []
-    for d in range(1, NZ):
-        block = req_mid.at[:, lax.rem(z + d, NZ)]
-        request_z.append(rcopy(block, req_recv.at[:, z], qzs.at[d - 1], qzr.at[d - 1], beside_z(d)))
-    for copy in request_z:
-        copy.start()
-    req_recv[:, z] = req_mid[:, z]
-    first = min(2, half)
-    for k in range(first):
-        ring_step(k)
 
     for copy in request_z:
         copy.wait_recv()
@@ -230,47 +223,53 @@
     table_copy.wait()
     high, low = small_parts(rq[...])
     chunk = NZ * TILE
-    diff_x = []
-    for d in range(nx):
-        side = lax.rem(x + d + 1, nx)
-        row = iota((chunk, 128), 0)
+    row = iota((chunk, 128), 0)
+    place = 2 * lax.rem(row, cap)
+    lanes = iota((chunk, 128), 1)
+    group = lax.div(lax.rem(iota((chunk, quarter), 0), TILE), cap)
+
+    def differences(side):
         spread = one_hot(lax.div(iota((chunk, ndp), 0), TILE) + side * NZ == iota((chunk, ndp), 1))
         wanted = dot(spread, high) * 16.0 + dot(spread, low)
-        place = 2 * lax.rem(row, cap)
-        lanes = iota((chunk, 128), 1)
         first_item = jnp.sum(jnp.where(lanes == place, wanted, 0.0), axis=1, keepdims=True)
         second_item = jnp.sum(jnp.where(lanes == place + 1, wanted, 0.0), axis=1, keepdims=True)
         items = iota((chunk, table.shape[0]), 1).astype(F32)
         signs = jnp.where(items == first_item, 1.0, 0.0) - jnp.where(items == second_item, 1.0, 0.0)
         signs = signs.astype(BF16)
-        group = lax.div(lax.rem(iota((chunk, quarter), 0), TILE), cap)
         total = jnp.zeros((chunk, quarter), F32)
         for g in range(4):
             term = dot(signs, table[:, g * quarter : (g + 1) * quarter])
             total = jnp.where(group == g, term, total)
-        total = total.astype(BF16).reshape(NZ, TILE, quarter)
-        if d + 1 < nx:
-            dsend[side] = total
-            diff_x.append(rcopy(dsend.at[side], dmid.at[x], dxs.at[d], dxr.at[d], beside_x(d + 1)))
-            diff_x[d].start()
-        else:
-            dmid[x] = total
-        if first + d < half:
-            ring_step(first + d)
+        return total.astype(BF16).reshape(NZ, TILE, quarter)
+
+    def along_z(hops, send, recv):
+        copies = []
+        for d in range(1, NZ):
+            block = dmid.at[hops, lax.rem(z + d, NZ)]
+            copies.append(rcopy(block, drecv.at[hops, z], send.at[d - 1], recv.at[d - 1], beside_z(d)))
+        for copy in copies:
+            copy.start()
+        drecv[hops, z] = dmid[hops, z]
+        return copies
+
+    dmid[0] = differences(x)
+    diff_z = along_z(pl.ds(0, 1), dzs, dzr)
+    diff_x = []
+    for d in range(1, nx):
+        side = lax.rem(x + d, nx)
+        dsend[side] = differences(side)
+        copy = rcopy(dsend.at[side], dmid.at[d], dxs.at[d - 1], dxr.at[d - 1], beside_x(d))
+        copy.start()
+        diff_x.append(copy)
+        if d - 1 < half:
+            ring_step(d - 1)
     y_forward(tok_copies)
-    first = first + nx
+    first = nx - 1
     if first < half:
         ring_step(first)
-
     for copy in diff_x:
         copy.wait_recv()
-    diff_z = []
-    for d in range(1, NZ):
-        block = dmid.at[:, lax.rem(z + d, NZ)]
-        diff_z.append(rcopy(block, drecv.at[:, z], dzs.at[d - 1], dzr.at[d - 1], beside_z(d)))
-    for copy in diff_z:
-        copy.start()
-    drecv[:, z] = dmid[:, z]
+    diff_z += along_z(pl.ds(1, nx - 1), ezs, ezr)
     for k in range(first + 1, half):
         ring_step(k)
     for copy in relays:
@@ -314,6 +313,9 @@
 
     def alive_of(block):
         return jnp.where(index + block * rows < length, 1.0, 0.0)
+
+    def block_span(block):
+        return pl.ds(pl.multiple_of(block * rows, rows), rows)
 
     def project(at, order):
         projected = dot(xn[at], w_head)
@@ -326,10 +328,11 @@
         copy = rcopy(kv.at[CORES * at + c], kv.at[CORES * at + c], ks.at[order], kr.at[order], sibling)
         copy.start()
         kv_copies.append(copy)
-        vt[CORES * at + c] = value.T.astype(BF16)
-        kt[CORES * at + c] = key.T.astype(BF16)
-        qs[at] = query.astype(BF16)
-        qt[at] = query.T.astype(BF16)
+        span = block_span(CORES * at + c)
+        vt[:, span] = value.T.astype(BF16)
+        kt[:, span] = key.T.astype(BF16)
+        qs[block_span(at), :] = query.astype(BF16)
+        qt[:, block_span(at)] = query.T.astype(BF16)
 
     project(y, 0)
     tok_copies[2].wait_recv()
@@ -346,8 +349,8 @@
     for u in range(HEADS):
         block = CORES * u + other
         both = kv[block].astype(F32)
-        vt[block] = both[:, :hd].T.astype(BF16)
-        kt[block] = both[:, hd:].T.astype(BF16)
+        vt[:, block_span(block)] = both[:, :hd].T.astype(BF16)
+        kt[:, block_span(block)] = both[:, hd:].T.astype(BF16)
 
     def send_when(t, src, dst, send, recv):
         @pl.when(y != t)
@@ -370,38 +373,31 @@
 
     causal = jnp.where(iota((rows, rows), 0) <= iota((rows, rows), 1), 1.0, 0.0)
     before = c.astype(F32)
-    for t in reversed(range(HEADS)):
-        total = jnp.zeros((hd, rows), F32)
+
+    def weigh(block, low, high, mask):
+        scores = dot(kv[block, :, hd:], qt[:, low:high]) * scale
+        sigma = jax.nn.sigmoid(scores)
+        weights = scores * sigma
+        change = (sigma + weights * (1.0 - sigma)) * (scale / history)
+        weights = weights * (1.0 / history)
+        if mask is not None:
+            weights, change = weights * mask, change * mask
+        wst[block_span(block), low:high] = weights.astype(BF16)
+        slope[block_span(block), low:high] = change
+
+    queries = HEADS * rows
+    for u in range(HEADS):
+        low, high = u * rows, (u + 1) * rows
         for parity in range(2):
-            for u in range(t + 1):
-                block = CORES * u + (c if parity == 0 else other)
-                scores = dot(kv[block, :, hd:], qt[t]) * scale
-                sigma = jax.nn.sigmoid(scores)
-                weights = scores * sigma
-                change = (sigma + weights * (1.0 - sigma)) * (scale / history)
-                weights = weights * (1.0 / history)
-                if u == t:
-                    mask = causal if parity == 0 else before
-                    weights, change = weights * mask, change * mask
-                weights = weights.astype(BF16)
-                wst[pair(t, u, parity)] = weights
-                slope[pair(t, u, parity)] = change
-                total = total + dot(vt[block], weights)
-        att_send[t] = total.T.astype(BF16)
-        send_when(t, att_send.at[t], att_recv.at[y], as_, ar)
+            block = CORES * u + (c if parity == 0 else other)
+            weigh(block, low, high, causal if parity == 0 else before)
+            if high < queries:
+                weigh(block, high, queries, None)
+        keys = CORES * (u + 1) * rows
+        att_send[u] = dot(vt[:, :keys], wst[:keys, low:high]).T.astype(BF16)
+        send_when(u, att_send.at[u], att_recv.at[y], as_, ar)
 
     relay_start(near_copies, near_relays)
-    y_forward(far_copies)
-    for copy in diff_z:
-        copy.wait_recv()
-    own_col = jnp.sum(
-        jnp.where(iota((rows, ndp), 1) == lax.div(iota((rows, ndp), 0), cap), own_row, 0), axis=1, keepdims=True
-    )
-    received = drecv[...].reshape(ndp * TILE, quarter)
-    source = own_col * TILE + lax.rem(index, cap)
-    for g in range(4):
-        pick = one_hot(iota((rows, ndp * TILE), 1) == source + g * cap)
-        idiff[:, g * quarter : (g + 1) * quarter] = dot(pick, received).astype(BF16)
     for copy in near_relays:
         copy.wait_recv()
     for t in range(HEADS):
@@ -415,6 +411,18 @@
             begin = side * (width // 2) + t * hd
             wout[:, begin : begin + hd] = dot(select, wall[t, :, :, :, :hd].reshape(width, hd)).astype(BF16)
 
+    y_forward(far_copies)
+    for copy in diff_z:
+        copy.wait_recv()
+    own_col = jnp.sum(
+        jnp.where(iota((rows, ndp), 1) == lax.div(iota((rows, ndp), 0), cap), own_row, 0), axis=1, keepdims=True
+    )
+    received = drecv[...].reshape(ndp * TILE, quarter)
+    hops = lax.rem(x - lax.div(own_col, NZ) + nx, nx)
+    source = (hops * NZ + lax.rem(own_col, NZ)) * TILE + lax.rem(index, cap)
+    for g in range(4):
+        pick = one_hot(iota((rows, ndp * TILE), 1) == source + g * cap)
+        idiff[:, g * quarter : (g + 1) * quarter] = dot(pick, received).astype(BF16)
     eye = iota((rows, rows), 0) == iota((rows, rows), 1)
     teacher = jnp.sum(jnp.where(eye, teach_ref[...], 0.0), axis=1, keepdims=True)
     alive = alive_of(sq)
@@ -453,23 +461,17 @@
     for t in range(HEADS):
         wait_when(t, da_recv.at[t], gs, gr)
     for t in range(HEADS):
-        dat[t] = da_recv[t].astype(F32).T.astype(BF16)
+        dat[:, t * rows : (t + 1) * rows] = da_recv[t].astype(F32).T.astype(BF16)
 
     def backward(u, parity):
         block = CORES * u + (c if parity == 0 else other)
-        grad_value = jnp.zeros((rows, hd), F32)
-        grad_key = jnp.zeros((rows, hd), F32)
-        for t in range(u, HEADS):
-            n = pair(t, u, parity)
-            grad_weights = dot(kv[block, :, :hd], dat[t])
-            grad_scores = (grad_weights * slope[n]).astype(BF16)
-            grad_value = grad_value + dot(wst[n], da_recv[t])
-            grad_key = grad_key + dot(grad_scores, qs[t])
-            term = dot(kt[block], grad_scores)
-            if parity == 1 and u == 0:
-                dqt[t] = term
-            else:
-                dqt[t] = dqt[t] + term
+        span, low = block_span(block), u * rows
+        grad_weights = dot(kv[block, :, :hd], dat[:, low:])
+        grad_scores = (grad_weights * slope[span, low:]).astype(BF16)
+        dst[span, low:] = grad_scores
+        grad_attended = da_recv[u:].reshape((HEADS - u) * rows, hd)
+        grad_value = dot(wst[span, low:], grad_attended)
+        grad_key = dot(grad_scores, qs[low:, :])
         return grad_value, grad_key
 
     part_copies = []
@@ -491,7 +493,8 @@
         keep = alive_of(CORES * u + c)
         grad_value = (grad_value + dvk_recv[u, :, :hd]) * keep
         grad_key = (grad_key + dvk_recv[u, :, hd:]) * keep
-        grad_query = dqt[u].T
+        keys = CORES * (u + 1) * rows
+        grad_query = dot(kt[:, :keys], dst[:keys, u * rows : (u + 1) * rows]).T
         gps[u, :, :hd] = (grad_value * silu_slope(proj[u, :, :hd])).astype(BF16)
         gps[u, :, hd : 2 * hd] = (grad_key * silu_slope(proj[u, :, hd : 2 * hd])).astype(BF16)
         gps[u, :, 2 * hd :] = (grad_query * silu_slope(proj[u, :, 2 * hd :])).astype(BF16)
@@ -545,7 +548,6 @@
     hw = gain_mid.shape[0]
     hd = hw // HEADS
     blocks = HEADS * CORES
-    pairs = HEADS * (HEADS + 1)
     half = NZ // 2
     quarter = width // 4
 
@@ -573,12 +575,12 @@
         vmem((rows, width), BF16),
         vmem((HEADS, rows, 3 * hd), F32),
         vmem((blocks, rows, 2 * hd), BF16),
-        vmem((blocks, hd, rows), BF16),
-        vmem((blocks, hd, rows), BF16),
-        vmem((HEADS, rows, hd), BF16),
-        vmem((HEADS, hd, rows), BF16),
-        vmem((pairs, rows, rows), BF16),
-        vmem((pairs, rows, rows), F32),
+        vmem((hd, blocks * rows), BF16),
+        vmem((hd, blocks * rows), BF16),
+        vmem((HEADS * rows, hd), BF16),
+        vmem((hd, HEADS * rows), BF16),
+        vmem((blocks * rows, HEADS * rows), BF16),
+        vmem((blocks * rows, HEADS * rows), F32),
         vmem((HEADS, rows, hd), BF16),
         vmem((HEADS, rows, hd), BF16),
         vmem((rows, hw), F32),
@@ -587,10 +589,10 @@
         vmem((rows, hw), BF16),
         vmem((HEADS, rows, hd), BF16),
         vmem((HEADS, rows, hd), BF16),
-        vmem((HEADS, hd, rows), BF16),
+        vmem((hd, HEADS * rows), BF16),
         vmem((HEADS, rows, 2 * hd), F32),
         vmem((HEADS, rows, 2 * hd), F32),
-        vmem((HEADS, hd, rows), F32),
+        vmem((blocks * rows, HEADS * rows), BF16),
         vmem((HEADS, rows, 3 * hd), BF16),
         vmem((HEADS, rows, 3 * hd), BF16),
         vmem((HEADS, 8, 128), F32),
@@ -604,7 +606,7 @@
         dma((half,)), dma((half,)),
         dma((6,)), dma((6,)),
         dma((nx,)), dma((nx,)), dma((NZ,)), dma((NZ,)),
-        dma((nx,)), dma((nx,)), dma((NZ,)), dma((NZ,)),
+        dma((nx,)), dma((nx,)), dma((NZ,)), dma((NZ,)), dma((NZ,)), dma((NZ,)),
         dma((6,)), dma((6,)), dma((3,)), dma((3,)),
         dma((6,)), dma((6,)), dma((3,)), dma((3,)),
         dma((HEADS,)), dma((HEADS,)),

time: 110 us -> 122 us (1.11); the launches traced: 108 us -> 122 us
  Pallas kernels: 104 us -> 117 us
    pallas_call x1, Pallas kernels: 104 us -> 117 us  [on_device(): pl.pallas_call(kernel, out_shape=(jax.ShapeDtypeStruct(tokens.shape, BF16...]
where the time goes in v3:
time: 122 us
  Pallas kernels  117 us (96%)
  between operations  2.34 us (2%)
  local copies, waits for them, and re-layouts  1.87 us (2%)
    pallas_call x1, Pallas kernels, on_device(): pl.pallas_call(kernel, out_shape=(jax.ShapeDtypeStruct(tokens.shape, BF16...  117 us

profile of v3, /device:TPU:25, one launch (start us, length us, event | category | flops | bytes accessed | tf_op | source)
XLA Modules:
  0.0 121.5 jit_solution(13678060507197133683)
XLA Ops:
  0.6 117.3 %shard_map.113 = (bf16[256,1024]{1,0:T(8,128)(2,1)}, f32[1,1]{1,0:T(1,128)}) custom-call(bf16[256,1024]{1,0:T(8,128)(2,1)} %tok_hbm.1, f32[1,256]{1,0:T(1,128)} %bitcast.10, s32[2,256]{1,0:T(2,128)} %bitcast.8, s32[1,64]{1,0:T(1,128)} %bitcast.11, s32[1,64]{1,0:T(1,128)} %bitcast.12, bf16[16,2048]{1,0:T(8,128)(2,1)} %wp_ref.1, bf16[8,1024]{1,0:T(8,128)(2,1)} %wo_hbm.1, ...), custom_call_target="tpu_custom_call" | custom-call | tf_op jit(solution)/shard_map/pallas_call | solution.py:621
  118.0 1.9 %copy.14 = bf16[256,1024]{1,0:T(8,128)(2,1)} copy(bf16[256,1024]{1,0:T(8,128)(2,1)} %get-tuple-element.8) | data formatting | bytes 1048576

commit v4 on v3

--- a/solution.py
+++ b/solution.py
@@ -58,10 +58,10 @@
     tok_hbm, teach_hbm, cand_hbm, own_hbm, len_hbm, wp_ref, wo_hbm, gin_hbm, gmid_hbm, table_hbm,
     out_ref, loss_ref,
     tok_ref, teach_ref, cand_ref, own_ref, len_ref, wo_ref, gin_ref, gmid_ref,
-    wall, xn, table, req_send, req_mid, req_recv, rq, dsend, dmid, drecv, idiff, proj, kv, kt, vt, qs, qt, wst, slope,
+    wall, piece, xn, table, req_send, req_mid, req_recv, rq, dsend, dmid, drecv, idiff, proj, kv, kt, vt, qs, qt, wst, slope,
     att_send, att_recv, gproj, wout, gout, gpg, da_send, da_recv, dat, dvk_send, dvk_recv, dst,
     gps, gpr, lby, lbc, lbx, lbz,
-    lsem, isem, xs, xr, zs, zr, rs, rr, ts, tr, qxs, qxr, qzs, qzr, dxs, dxr, dzs, dzr, ezs, ezr,
+    lsem, isem, xs, xr, zs, zr, rs, rr, ts, tr, qxs, qxr, qzs, qzr, dxs, dxr, dzs, dzr,
     ws, wr, wrs, wrr, vs, vr, vrs, vrr, ks, kr, as_, ar, gs, gr, ps, pr, fs, fr, lys, lyr, lcs, lcr, lxs, lxr, lzs, lzr,
 ):
     rows, width = tok_ref.shape
@@ -80,7 +80,6 @@
     x, z = lax.div(dp, NZ), lax.rem(dp, NZ)
     y, c = lax.div(sq, CORES), lax.rem(sq, CORES)
     other = 1 - c
-    way = 1 - 2 * c
     yp, ym = lax.rem(y + 1, HEADS), lax.rem(y + HEADS - 1, HEADS)
     yo = lax.rem(y + 2, HEADS)
     up, down = (dp, yp * CORES + c), (dp, ym * CORES + c)
@@ -103,6 +102,7 @@
     barrier = pltpu.get_barrier_semaphore()
     partners = [sibling] + [beside_y(d) for d in range(1, HEADS)]
     partners += [beside_x(d) for d in range(1, nx)] + [beside_z(d) for d in range(1, NZ)]
+    partners += [(device, y * CORES + other) for device, _ in [beside_z(d) for d in range(1, NZ)]]
     for device in partners:
         pl.semaphore_signal(barrier, inc=1, device_id=device, device_id_type=MESH)
 
@@ -117,18 +117,36 @@
     for i, (start, to) in enumerate(pieces):
         begin = pl.multiple_of(start + y * hd, hd)
         local.append(
-            pltpu.make_async_copy(wp_ref.at[:, pl.ds(begin, hd)], wall.at[y, x, z, :, pl.ds(to, hd)], lsem.at[i])
+            pltpu.make_async_copy(wp_ref.at[:, pl.ds(begin, hd)], piece.at[:, pl.ds(to, hd)], lsem.at[i])
         )
     table_copy = pltpu.make_async_copy(table_hbm, table, lsem.at[4])
     for copy in inputs + local:
         copy.start()
     table_copy.start()
-    for copy in inputs:
+    for copy in inputs + local:
         copy.wait()
-
-    tokens = tok_ref[...].astype(F32)
-    normed_raw, factor_in = normalize(tokens)
-    xn[y] = (normed_raw * gin_ref[...]).astype(BF16)
+    sides = [wo_ref[:, pl.ds(pl.multiple_of(i * (width // 2) + y * hd, hd), hd)].astype(F32) for i in range(2)]
+    piece[:, :hd] = jnp.concatenate(sides, axis=0).astype(BF16)
+
+    @pl.when(c == lax.div(z, half))
+    def _():
+        wall[y, x, z] = piece[...]
+
+    pl.semaphore_wait(barrier, len(partners))
+
+    shard = wall.at[y, x, z]
+    collector = y * CORES + lax.div(z, half)
+
+    def shard_copy(i):
+        device = (x * NZ + lax.rem(z + 1 + i + c * half, NZ), collector)
+        return rcopy(piece, shard, zs.at[i], zr.at[lax.rem(z, half)], device)
+
+    for i in range(half - 1):
+        shard_copy(i).start()
+
+    @pl.when(c == 0)
+    def _():
+        shard_copy(half - 1).start()
 
     own_row = own_ref[...]
     expand = one_hot(lax.div(iota((ndp, rows), 1), cap) == iota((ndp, rows), 0))
@@ -141,12 +159,17 @@
     requests = dot_nt(to_owner, high) * 16.0 + dot_nt(to_owner, low)
     for p in range(ndp):
         req_send[p // NZ, p % NZ] = requests[p : p + 1, :]
-    sides = [wo_ref[:, pl.ds(pl.multiple_of(i * (width // 2) + y * hd, hd), hd)].astype(F32) for i in range(2)]
-    wall[y, x, z, :, :hd] = jnp.concatenate(sides, axis=0).astype(BF16)
-
-    for copy in local:
-        copy.wait()
-    pl.semaphore_wait(barrier, len(partners))
+    request_x = []
+    for d in range(1, nx):
+        block = req_send.at[lax.rem(x + d, nx)]
+        request_x.append(rcopy(block, req_mid.at[x], qxs.at[d - 1], qxr.at[d - 1], beside_x(d)))
+    for copy in request_x:
+        copy.start()
+    req_mid[x] = req_send[x]
+
+    tokens = tok_ref[...].astype(F32)
+    normed_raw, factor_in = normalize(tokens)
+    xn[y] = (normed_raw * gin_ref[...]).astype(BF16)
 
     def y_copies(part, send, recv):
         return [
@@ -170,18 +193,6 @@
 
     tok_copies = y_copies(lambda at, h: xn.at[at, pl.ds(h * (rows // 2), rows // 2), :], ts, tr)
 
-    request_x = []
-    for d in range(1, nx):
-        block = req_send.at[lax.rem(x + d, nx)]
-        request_x.append(rcopy(block, req_mid.at[x], qxs.at[d - 1], qxr.at[d - 1], beside_x(d)))
-    for copy in request_x:
-        copy.start()
-    req_mid[x] = req_send[x]
-    x_copies = []
-    for d in range(1, nx):
-        copy = rcopy(wall.at[y, x, z], wall.at[y, x, z], xs.at[d - 1], xr.at[d - 1], beside_x(d))
-        copy.start()
-        x_copies.append(copy)
     y_start(tok_copies)
 
     for copy in request_x:
@@ -194,27 +205,22 @@
         copy.start()
     req_recv[:, z] = req_mid[:, z]
 
-    def at_z(distance):
-        return lax.rem(z - way * distance + NZ, NZ)
-
-    ahead = (x * NZ + lax.rem(z + way + NZ, NZ), sq)
-    z_copies, relays = [], []
-    for k in range(half):
-        src = wall.at[y, :, at_z(k)]
-        z_copies.append(rcopy(src, src, zs.at[k], zr.at[k], ahead))
-        if k < half - 1:
-            got = wall.at[y, :, at_z(k + 1)]
-            relays.append(rcopy(got, got, rs.at[k], rr.at[k], sibling))
-
-    def ring_step(k):
-        z_copies[k].wait_recv()
-        if k + 1 < half:
-            z_copies[k + 1].start()
-            relays[k].start()
-
+    def collected(d):
+        return wall.at[y, lax.rem(x - d + nx, nx), pl.ds(c * half, half)]
+
+    for j in range(half):
+
+        @pl.when(z != c * half + j)
+        def _():
+            rcopy(shard, shard, zs.at[0], zr.at[j], sibling).wait_recv()
+
+    x_copies = []
+    for d in range(1, nx):
+        x_copies.append(rcopy(collected(0), collected(0), xs.at[d - 1], xr.at[d - 1], beside_x(d)))
+    relays = [rcopy(collected(d), collected(d), rs.at[d], rr.at[d], sibling) for d in range(nx)]
     for copy in x_copies:
-        copy.wait_recv()
-    z_copies[0].start()
+        copy.start()
+    relays[0].start()
 
     for copy in request_z:
         copy.wait_recv()
@@ -242,18 +248,6 @@
             total = jnp.where(group == g, term, total)
         return total.astype(BF16).reshape(NZ, TILE, quarter)
 
-    def along_z(hops, send, recv):
-        copies = []
-        for d in range(1, NZ):
-            block = dmid.at[hops, lax.rem(z + d, NZ)]
-            copies.append(rcopy(block, drecv.at[hops, z], send.at[d - 1], recv.at[d - 1], beside_z(d)))
-        for copy in copies:
-            copy.start()
-        drecv[hops, z] = dmid[hops, z]
-        return copies
-
-    dmid[0] = differences(x)
-    diff_z = along_z(pl.ds(0, 1), dzs, dzr)
     diff_x = []
     for d in range(1, nx):
         side = lax.rem(x + d, nx)
@@ -261,17 +255,21 @@
         copy = rcopy(dsend.at[side], dmid.at[d], dxs.at[d - 1], dxr.at[d - 1], beside_x(d))
         copy.start()
         diff_x.append(copy)
-        if d - 1 < half:
-            ring_step(d - 1)
+    dmid[0] = differences(x)
+    for d in range(1, nx):
+        x_copies[d - 1].wait_recv()
+        relays[d].start()
+
+    for copy in diff_x:
+        copy.wait_recv()
+    diff_z = []
+    for d in range(1, NZ):
+        block = dmid.at[:, lax.rem(z + d, NZ)]
+        diff_z.append(rcopy(block, drecv.at[:, z], dzs.at[d - 1], dzr.at[d - 1], beside_z(d)))
+    for copy in diff_z:
+        copy.start()
+    drecv[:, z] = dmid[:, z]
     y_forward(tok_copies)
-    first = nx - 1
-    if first < half:
-        ring_step(first)
-    for copy in diff_x:
-        copy.wait_recv()
-    diff_z += along_z(pl.ds(1, nx - 1), ezs, ezr)
-    for k in range(first + 1, half):
-        ring_step(k)
     for copy in relays:
         copy.wait_recv()
 
@@ -402,11 +400,11 @@
         copy.wait_recv()
     for t in range(HEADS):
         gproj[:, t * hd : (t + 1) * hd] = dot(xn[y], wall[t, :, :, :, hd : 2 * hd].reshape(width, hd))
-    shard = TILE // 2
+    lines = TILE // 2
     line, spot = iota((hw, width), 0), iota((hw, width), 1)
-    origin = lax.div(line, shard) * TILE + lax.rem(line, shard)
+    origin = lax.div(line, lines) * TILE + lax.rem(line, lines)
     for side in range(2):
-        select = one_hot(spot == origin + side * shard)
+        select = one_hot(spot == origin + side * lines)
         for t in range(HEADS):
             begin = side * (width // 2) + t * hd
             wout[:, begin : begin + hd] = dot(select, wall[t, :, :, :, :hd].reshape(width, hd)).astype(BF16)
@@ -527,7 +525,14 @@
         copy.wait_recv()
     loss_ref[...] = jnp.sum(lbz[...], axis=0)[0:1, 0:1] / live_total
 
-    for copy in x_copies + z_copies + relays + tok_copies + near_copies + near_relays + far_copies + far_relays:
+    for i in range(half - 1):
+        shard_copy(i).wait_send()
+
+    @pl.when(c == 0)
+    def _():
+        shard_copy(half - 1).wait_send()
+
+    for copy in x_copies + relays + tok_copies + near_copies + near_relays + far_copies + far_relays:
         copy.wait_send()
     for copy in kv_copies + part_copies + loss_y + loss_c + loss_x + loss_z:
         copy.wait_send()
@@ -563,6 +568,7 @@
         vmem((1, width), F32),
         vmem((1, hw), F32),
         vmem((HEADS, nx, NZ, TILE, 5 * hd), BF16),
+        vmem((TILE, 5 * hd), BF16),
         vmem((HEADS, rows, width), BF16),
         vmem(item_table.shape, BF16),
         vmem((nx, NZ, 1, 128), F32),
@@ -603,10 +609,10 @@
         dma((8,)),
         dma((nx,)), dma((nx,)),
         dma((half,)), dma((half,)),
-        dma((half,)), dma((half,)),
+        dma((nx,)), dma((nx,)),
         dma((6,)), dma((6,)),
         dma((nx,)), dma((nx,)), dma((NZ,)), dma((NZ,)),
-        dma((nx,)), dma((nx,)), dma((NZ,)), dma((NZ,)), dma((NZ,)), dma((NZ,)),
+        dma((nx,)), dma((nx,)), dma((NZ,)), dma((NZ,)),
         dma((6,)), dma((6,)), dma((3,)), dma((3,)),
         dma((6,)), dma((6,)), dma((3,)), dma((3,)),
         dma((HEADS,)), dma((HEADS,)),

time: 122 us -> 103 us (0.84); the launches traced: 122 us -> 101 us
  Pallas kernels: 117 us -> 96.8 us
    pallas_call x1, Pallas kernels: 117 us -> 96.8 us  [on_device(): pl.pallas_call(kernel, out_shape=(jax.ShapeDtypeStruct(tokens.shape, BF16...]
where the time goes in v4:
time: 103 us; the launch traced here: 101 us
  Pallas kernels  96.8 us (94%)
  between operations  2.34 us (2%)
  local copies, waits for them, and re-layouts  1.87 us (2%)
    pallas_call x1, Pallas kernels, on_device(): pl.pallas_call(kernel, out_shape=(jax.ShapeDtypeStruct(tokens.shape, BF16...  96.8 us

profile of v4, /device:TPU:25, one launch (start us, length us, event | category | flops | bytes accessed | tf_op | source)
XLA Modules:
  0.0 101.0 jit_solution(1026790322648710154)
XLA Ops:
  0.6 96.8 %shard_map.113 = (bf16[256,1024]{1,0:T(8,128)(2,1)}, f32[1,1]{1,0:T(1,128)}) custom-call(bf16[256,1024]{1,0:T(8,128)(2,1)} %tok_hbm.1, f32[1,256]{1,0:T(1,128)} %bitcast.10, s32[2,256]{1,0:T(2,128)} %bitcast.8, s32[1,64]{1,0:T(1,128)} %bitcast.11, s32[1,64]{1,0:T(1,128)} %bitcast.12, bf16[16,2048]{1,0:T(8,128)(2,1)} %wp_ref.1, bf16[8,1024]{1,0:T(8,128)(2,1)} %wo_hbm.1, ...), custom_call_target="tpu_custom_call" | custom-call | tf_op jit(solution)/shard_map/pallas_call | solution.py:627
  97.4 1.9 %copy.14 = bf16[256,1024]{1,0:T(8,128)(2,1)} copy(bf16[256,1024]{1,0:T(8,128)(2,1)} %get-tuple-element.8) | data formatting | bytes 1048576

commit v5 on v4

--- a/solution.py
+++ b/solution.py
@@ -58,7 +58,7 @@
     tok_hbm, teach_hbm, cand_hbm, own_hbm, len_hbm, wp_ref, wo_hbm, gin_hbm, gmid_hbm, table_hbm,
     out_ref, loss_ref,
     tok_ref, teach_ref, cand_ref, own_ref, len_ref, wo_ref, gin_ref, gmid_ref,
-    wall, piece, xn, table, req_send, req_mid, req_recv, rq, dsend, dmid, drecv, idiff, proj, kv, kt, vt, qs, qt, wst, slope,
+    wall, piece, xn, table, req_send, req_mid, req_recv, rq, dsend, dmid, drecv, picks, idiff, proj, kv, kt, vt, qs, qt, wst, slope,
     att_send, att_recv, gproj, wout, gout, gpg, da_send, da_recv, dat, dvk_send, dvk_recv, dst,
     gps, gpr, lby, lbc, lbx, lbz,
     lsem, isem, xs, xr, zs, zr, rs, rr, ts, tr, qxs, qxr, qzs, qzr, dxs, dxr, dzs, dzr,
@@ -248,28 +248,42 @@
             total = jnp.where(group == g, term, total)
         return total.astype(BF16).reshape(NZ, TILE, quarter)
 
+    hops = [0, 1] + [nx - 1] * (nx > 2) + list(range(2, nx - 1))
+    rounds = [(0, 1), (1, min(3, nx))] + [(3, nx)] * (nx > 3)
+    diff_z = []
+
+    def along_z(i):
+        low, high = rounds[i]
+        slots = pl.ds(low, high - low)
+        copies = []
+        for d in range(1, NZ):
+            block = dmid.at[slots, lax.rem(z + d, NZ)]
+            copies.append(rcopy(block, drecv.at[slots, z], dzs.at[i, d - 1], dzr.at[i, d - 1], beside_z(d)))
+        for copy in copies:
+            copy.start()
+        drecv[slots, z] = dmid[slots, z]
+        diff_z.extend(copies)
+
+    dmid[0] = differences(x)
+    along_z(0)
     diff_x = []
-    for d in range(1, nx):
+    for slot in range(1, nx):
+        d = hops[slot]
         side = lax.rem(x + d, nx)
         dsend[side] = differences(side)
-        copy = rcopy(dsend.at[side], dmid.at[d], dxs.at[d - 1], dxr.at[d - 1], beside_x(d))
+        copy = rcopy(dsend.at[side], dmid.at[slot], dxs.at[slot - 1], dxr.at[slot - 1], beside_x(d))
         copy.start()
         diff_x.append(copy)
-    dmid[0] = differences(x)
+        if slot == 1:
+            y_forward(tok_copies)
+
     for d in range(1, nx):
-        x_copies[d - 1].wait_recv()
-        relays[d].start()
-
-    for copy in diff_x:
-        copy.wait_recv()
-    diff_z = []
-    for d in range(1, NZ):
-        block = dmid.at[:, lax.rem(z + d, NZ)]
-        diff_z.append(rcopy(block, drecv.at[:, z], dzs.at[d - 1], dzr.at[d - 1], beside_z(d)))
-    for copy in diff_z:
-        copy.start()
-    drecv[:, z] = dmid[:, z]
-    y_forward(tok_copies)
+        if d < len(rounds):
+            for slot in range(*rounds[d]):
+                diff_x[slot - 1].wait_recv()
+            along_z(d)
+        x_copies[hops[d] - 1].wait_recv()
+        relays[hops[d]].start()
     for copy in relays:
         copy.wait_recv()
 
@@ -410,17 +424,20 @@
             wout[:, begin : begin + hd] = dot(select, wall[t, :, :, :, :hd].reshape(width, hd)).astype(BF16)
 
     y_forward(far_copies)
-    for copy in diff_z:
-        copy.wait_recv()
     own_col = jnp.sum(
         jnp.where(iota((rows, ndp), 1) == lax.div(iota((rows, ndp), 0), cap), own_row, 0), axis=1, keepdims=True
     )
+    away = lax.rem(x - lax.div(own_col, NZ) + nx, nx)
+    slot_of = sum(jnp.where(away == hop, slot, 0) for slot, hop in enumerate(hops))
+    source = (slot_of * NZ + lax.rem(own_col, NZ)) * TILE + lax.rem(index, cap)
+    for g in range(4):
+        picks[g] = one_hot(iota((rows, ndp * TILE), 1) == source + g * cap)
+    for copy in diff_z:
+        copy.wait_recv()
     received = drecv[...].reshape(ndp * TILE, quarter)
-    hops = lax.rem(x - lax.div(own_col, NZ) + nx, nx)
-    source = (hops * NZ + lax.rem(own_col, NZ)) * TILE + lax.rem(index, cap)
     for g in range(4):
-        pick = one_hot(iota((rows, ndp * TILE), 1) == source + g * cap)
-        idiff[:, g * quarter : (g + 1) * quarter] = dot(pick, received).astype(BF16)
+        idiff[:, g * quarter : (g + 1) * quarter] = dot(picks[g], received).astype(BF16)
+
     eye = iota((rows, rows), 0) == iota((rows, rows), 1)
     teacher = jnp.sum(jnp.where(eye, teach_ref[...], 0.0), axis=1, keepdims=True)
     alive = alive_of(sq)
@@ -578,6 +595,7 @@
         vmem((nx, NZ, TILE, quarter), BF16),
         vmem((nx, NZ, TILE, quarter), BF16),
         vmem((nx, NZ, TILE, quarter), BF16),
+        vmem((4, rows, ndp * TILE), BF16),
         vmem((rows, width), BF16),
         vmem((HEADS, rows, 3 * hd), F32),
         vmem((blocks, rows, 2 * hd), BF16),
@@ -612,7 +630,7 @@
         dma((nx,)), dma((nx,)),
         dma((6,)), dma((6,)),
         dma((nx,)), dma((nx,)), dma((NZ,)), dma((NZ,)),
-        dma((nx,)), dma((nx,)), dma((NZ,)), dma((NZ,)),
+        dma((nx,)), dma((nx,)), dma((3, NZ)), dma((3, NZ)),
         dma((6,)), dma((6,)), dma((3,)), dma((3,)),
         dma((6,)), dma((6,)), dma((3,)), dma((3,)),
         dma((HEADS,)), dma((HEADS,)),

time: 103 us -> 99.3 us (0.964); the launches traced: 101 us -> 98.4 us
  Pallas kernels: 96.8 us -> 94.2 us
    pallas_call x1, Pallas kernels: 96.8 us -> 94.2 us  [on_device(): pl.pallas_call(kernel, out_shape=(jax.ShapeDtypeStruct(tokens.shape, BF16...]
where the time goes in v5:
time: 99.3 us; the launch traced here: 98.4 us
  Pallas kernels  94.2 us (95%)
  between operations  2.34 us (2%)
  local copies, waits for them, and re-layouts  1.87 us (2%)
    pallas_call x1, Pallas kernels, on_device(): pl.pallas_call(kernel, out_shape=(jax.ShapeDtypeStruct(tokens.shape, BF16...  94.2 us

profile of v5, /device:TPU:25, one launch (start us, length us, event | category | flops | bytes accessed | tf_op | source)
XLA Modules:
  0.0 98.4 jit_solution(4593205710875949958)
XLA Ops:
  0.6 94.2 %shard_map.113 = (bf16[256,1024]{1,0:T(8,128)(2,1)}, f32[1,1]{1,0:T(1,128)}) custom-call(bf16[256,1024]{1,0:T(8,128)(2,1)} %tok_hbm.1, f32[1,256]{1,0:T(1,128)} %bitcast.10, s32[2,256]{1,0:T(2,128)} %bitcast.8, s32[1,64]{1,0:T(1,128)} %bitcast.11, s32[1,64]{1,0:T(1,128)} %bitcast.12, bf16[16,2048]{1,0:T(8,128)(2,1)} %wp_ref.1, bf16[8,1024]{1,0:T(8,128)(2,1)} %wo_hbm.1, ...), custom_call_target="tpu_custom_call" | custom-call | tf_op jit(solution)/shard_map/pallas_call | solution.py:645
  94.8 1.9 %copy.14 = bf16[256,1024]{1,0:T(8,128)(2,1)} copy(bf16[256,1024]{1,0:T(8,128)(2,1)} %get-tuple-element.8) | data formatting | bytes 1048576

commit v6 on v5

--- a/solution.py
+++ b/solution.py
@@ -277,28 +277,17 @@
         if slot == 1:
             y_forward(tok_copies)
 
-    for d in range(1, nx):
-        if d < len(rounds):
-            for slot in range(*rounds[d]):
-                diff_x[slot - 1].wait_recv()
-            along_z(d)
-        x_copies[hops[d] - 1].wait_recv()
-        relays[hops[d]].start()
-    for copy in relays:
-        copy.wait_recv()
-
     near = pl.ds(0, 2 * hd)
     far = pl.ds(2 * hd, 3 * hd)
-    per_core = nx // CORES
 
     def weight_part(columns):
         def part(at, h):
-            return wall.at[at, pl.ds(c * per_core, per_core), pl.ds(h * half, half), :, columns]
+            return wall.at[at, pl.ds(h * (nx // 2), nx // 2), pl.ds(c * half, half), :, columns]
 
         return part
 
     def weight_relay(at, index, columns, send, recv):
-        block = wall.at[at, pl.ds(c * per_core, per_core), :, :, columns]
+        block = wall.at[at, :, pl.ds(c * half, half), :, columns]
         return rcopy(block, block, send.at[index], recv.at[index], sibling)
 
     near_copies = y_copies(weight_part(near), ws, wr)
@@ -315,7 +304,18 @@
         copies[5].wait_recv()
         relayed[2].start()
 
+    for d in hops[1:]:
+        x_copies[d - 1].wait_recv()
+        relays[d].start()
     y_start(near_copies)
+
+    for d in range(1, nx):
+        if d < len(rounds):
+            for slot in range(*rounds[d]):
+                diff_x[slot - 1].wait_recv()
+            along_z(d)
+    for copy in relays:
+        copy.wait_recv()
 
     length = jnp.sum(jnp.where(iota((1, ndp), 1) == dp, len_ref[...], 0), axis=1, keepdims=True)
     live_total = jnp.sum(len_ref[...], axis=1, keepdims=True).astype(F32)

time: 99.3 us -> 94.3 us (0.950)
  Pallas kernels: 94.2 us -> 89.4 us
    pallas_call x1, Pallas kernels: 94.2 us -> 89.4 us  [on_device(): pl.pallas_call(kernel, out_shape=(jax.ShapeDtypeStruct(tokens.shape, BF16...]
where the time goes in v6:
time: 94.3 us; the launch traced here: 93.7 us
  Pallas kernels  89.4 us (95%)
  between operations  2.34 us (2%)
  local copies, waits for them, and re-layouts  1.87 us (2%)
    pallas_call x1, Pallas kernels, on_device(): pl.pallas_call(kernel, out_shape=(jax.ShapeDtypeStruct(tokens.shape, BF16...  89.4 us

profile of v6, /device:TPU:25, one launch (start us, length us, event | category | flops | bytes accessed | tf_op | source)
XLA Modules:
  0.0 93.7 jit_solution(7806851317049752387)
XLA Ops:
  0.6 89.4 %shard_map.113 = (bf16[256,1024]{1,0:T(8,128)(2,1)}, f32[1,1]{1,0:T(1,128)}) custom-call(bf16[256,1024]{1,0:T(8,128)(2,1)} %tok_hbm.1, f32[1,256]{1,0:T(1,128)} %bitcast.10, s32[2,256]{1,0:T(2,128)} %bitcast.8, s32[1,64]{1,0:T(1,128)} %bitcast.11, s32[1,64]{1,0:T(1,128)} %bitcast.12, bf16[16,2048]{1,0:T(8,128)(2,1)} %wp_ref.1, bf16[8,1024]{1,0:T(8,128)(2,1)} %wo_hbm.1, ...), custom_call_target="tpu_custom_call" | custom-call | tf_op jit(solution)/shard_map/pallas_call | solution.py:645
  90.1 1.9 %copy.14 = bf16[256,1024]{1,0:T(8,128)(2,1)} copy(bf16[256,1024]{1,0:T(8,128)(2,1)} %get-tuple-element.8) | data formatting | bytes 1048576

commit v7 on v6

--- a/solution.py
+++ b/solution.py
@@ -264,6 +264,33 @@
         drecv[slots, z] = dmid[slots, z]
         diff_z.extend(copies)
 
+    near = pl.ds(0, 2 * hd)
+    far = pl.ds(2 * hd, 3 * hd)
+
+    def weight_part(columns):
+        def part(at, h):
+            return wall.at[at, pl.ds(h * (nx // 2), nx // 2), pl.ds(c * half, half), :, columns]
+
+        return part
+
+    def weight_relay(at, index, columns, send, recv):
+        block = wall.at[at, :, pl.ds(c * half, half), :, columns]
+        return rcopy(block, block, send.at[index], recv.at[index], sibling)
+
+    near_copies = y_copies(weight_part(near), ws, wr)
+    near_relays = [weight_relay(at, i, near, wrs, wrr) for i, at in enumerate((ym, yp, yo))]
+    far_copies = y_copies(weight_part(far), vs, vr)
+    far_relays = [weight_relay(at, i, far, vrs, vrr) for i, at in enumerate((ym, yp, yo))]
+
+    def relay_start(copies, relayed):
+        copies[2].wait_recv()
+        relayed[0].start()
+        copies[3].wait_recv()
+        relayed[1].start()
+        copies[4].wait_recv()
+        copies[5].wait_recv()
+        relayed[2].start()
+
     dmid[0] = differences(x)
     along_z(0)
     diff_x = []
@@ -276,38 +303,10 @@
         diff_x.append(copy)
         if slot == 1:
             y_forward(tok_copies)
-
-    near = pl.ds(0, 2 * hd)
-    far = pl.ds(2 * hd, 3 * hd)
-
-    def weight_part(columns):
-        def part(at, h):
-            return wall.at[at, pl.ds(h * (nx // 2), nx // 2), pl.ds(c * half, half), :, columns]
-
-        return part
-
-    def weight_relay(at, index, columns, send, recv):
-        block = wall.at[at, :, pl.ds(c * half, half), :, columns]
-        return rcopy(block, block, send.at[index], recv.at[index], sibling)
-
-    near_copies = y_copies(weight_part(near), ws, wr)
-    near_relays = [weight_relay(at, i, near, wrs, wrr) for i, at in enumerate((ym, yp, yo))]
-    far_copies = y_copies(weight_part(far), vs, vr)
-    far_relays = [weight_relay(at, i, far, vrs, vrr) for i, at in enumerate((ym, yp, yo))]
-
-    def relay_start(copies, relayed):
-        copies[2].wait_recv()
-        relayed[0].start()
-        copies[3].wait_recv()
-        relayed[1].start()
-        copies[4].wait_recv()
-        copies[5].wait_recv()
-        relayed[2].start()
-
-    for d in hops[1:]:
-        x_copies[d - 1].wait_recv()
-        relays[d].start()
-    y_start(near_copies)
+            for d in hops[1:]:
+                x_copies[d - 1].wait_recv()
+                relays[d].start()
+            y_start(near_copies)
 
     for d in range(1, nx):
         if d < len(rounds):

time: 94.3 us -> 94.8 us (level)
  Pallas kernels: 89.4 us -> 90.4 us
    pallas_call x1, Pallas kernels: 89.4 us -> 90.4 us  [on_device(): pl.pallas_call(kernel, out_shape=(jax.ShapeDtypeStruct(tokens.shape, BF16...]
where the time goes in v7:
time: 94.8 us; the launch traced here: 94.6 us
  Pallas kernels  90.4 us (95%)
  between operations  2.34 us (2%)
  local copies, waits for them, and re-layouts  1.87 us (2%)
    pallas_call x1, Pallas kernels, on_device(): pl.pallas_call(kernel, out_shape=(jax.ShapeDtypeStruct(tokens.shape, BF16...  90.4 us

profile of v7, /device:TPU:25, one launch (start us, length us, event | category | flops | bytes accessed | tf_op | source)
XLA Modules:
  0.0 94.6 jit_solution(9798287845194239506)
XLA Ops:
  0.6 90.4 %shard_map.113 = (bf16[256,1024]{1,0:T(8,128)(2,1)}, f32[1,1]{1,0:T(1,128)}) custom-call(bf16[256,1024]{1,0:T(8,128)(2,1)} %tok_hbm.1, f32[1,256]{1,0:T(1,128)} %bitcast.10, s32[2,256]{1,0:T(2,128)} %bitcast.8, s32[1,64]{1,0:T(1,128)} %bitcast.11, s32[1,64]{1,0:T(1,128)} %bitcast.12, bf16[16,2048]{1,0:T(8,128)(2,1)} %wp_ref.1, bf16[8,1024]{1,0:T(8,128)(2,1)} %wo_hbm.1, ...), custom_call_target="tpu_custom_call" | custom-call | tf_op jit(solution)/shard_map/pallas_call | solution.py:644
  91.1 1.9 %copy.14 = bf16[256,1024]{1,0:T(8,128)(2,1)} copy(bf16[256,1024]{1,0:T(8,128)(2,1)} %get-tuple-element.8) | data formatting | bytes 1048576
